TPU v7x, 1024 devices: a whole 4x4x32 slice. The times are simulated.
1024 devices in a mesh: expert: 64 (over z, core), tensor: 16 (over y, x).
Axes of the slice: x: 4, y: 4, z: 32, core: 2. Of those that a mesh axis runs over, the one named last changes fastest.
Arguments:
- tokens: bfloat16 [1536, 4096], P('expert', 'tensor'), may hold values from -6 to 6
- routes: int32 [1536, 8], P('expert'), may hold values from 0 to 63, all different within a row; in each aligned block of 24 rows (0 to 23, 24 to 47, ...) at most 4 rows name the same one
- gates: float32 [1536, 8], P('expert'), may hold values from 0.1 to 1
- cotangent: bfloat16 [1536, 4096], P('expert', 'tensor'), may hold values from -6 to 6
- w_gate: bfloat16 [64, 768, 4096], P('expert', 'tensor'), may hold values from -0.09375 to 0.09375
- w_up: bfloat16 [64, 768, 4096], P('expert', 'tensor'), may hold values from -0.09375 to 0.09375
- w_down: bfloat16 [64, 768, 4096], P('expert', 'tensor'), may hold values from -0.21875 to 0.21875
Outputs:
- mixed: bfloat16 [1536, 4096], P('expert', 'tensor')
- token_grad: bfloat16 [1536, 4096], P('expert', 'tensor')
- gate_grad: bfloat16 [64, 768, 4096], P('expert', 'tensor')
- up_grad: bfloat16 [64, 768, 4096], P('expert', 'tensor')
- down_grad: bfloat16 [64, 768, 4096], P('expert', 'tensor')
Inputs may be any that keep to these rules, and one draw needn't show every extreme that they name: `routes`: each row names 8 different experts. Among the 24 rows of one index of the expert axis, no expert is named by more than 4 rows, a bound that some block reaches.
All inputs are finite; a program needn't handle non-finite values.
Results may differ from a plain program's by a relative error of at most 0.02.
Values may be sent and summed in bfloat16 or wider, within the bound.
No kernel may reach another device: no remote copies, remote signals or barrier semaphores. Data moves between devices by JAX's collectives and lax.ppermute only.
A program may use at most 32 MiB of HBM per device.

v0:
```python
import jax
import jax.numpy as jnp
from jax import lax
from jax.sharding import PartitionSpec as P

CAP = 4


def silu_pair(values):
    sigmoid = jax.nn.sigmoid(values)
    return (values * sigmoid, sigmoid * (1.0 + values * (1.0 - sigmoid)))


def shards(tokens, routes, gates, cotangent, w_gate, w_up, w_down):
    expert_count = w_gate.shape[0] * lax.axis_size("expert")
    slot_count = expert_count * CAP
    listed = routes.reshape(-1)
    labels = jnp.arange(expert_count, dtype=jnp.int32)
    onehot = (listed[:, None] == labels[None, :]).astype(jnp.int32)
    earlier = jnp.cumsum(onehot, axis=0) - onehot
    position = jnp.sum(earlier * onehot, axis=1)
    slot_of = (listed * CAP + position).reshape(routes.shape)
    matches = slot_of[:, :, None] == jnp.arange(slot_count, dtype=jnp.int32)[None, None, :]
    selector = jnp.sum(matches.astype(jnp.float32), axis=1).T.astype(jnp.bfloat16)
    blending = jnp.sum(jnp.where(matches, gates[:, :, None], 0.0), axis=1)
    blend_cols = blending.T

    def place_tokens(source):
        return jnp.dot(selector, source, preferred_element_type=jnp.float32).astype(jnp.bfloat16)

    def place_weighted(source):
        return jnp.dot(
            blend_cols, source.astype(jnp.float32), precision=lax.Precision.HIGHEST
        ).astype(jnp.bfloat16)

    def to_experts(source, builder):
        complete = lax.all_gather(source, "tensor", axis=1, tiled=True)
        buffer = builder(complete).reshape(expert_count, CAP, complete.shape[1])
        return lax.all_to_all(buffer, "expert", split_axis=0, concat_axis=1, tiled=True)

    def from_experts(partial_value):
        summed = lax.psum_scatter(
            partial_value.astype(jnp.bfloat16), "tensor", scatter_dimension=2, tiled=True
        )
        returned = lax.all_to_all(summed, "expert", split_axis=1, concat_axis=0, tiled=True)
        return returned.reshape(slot_count, returned.shape[2])

    inputs = to_experts(tokens, place_tokens)
    gate_pre = jnp.einsum("erd,efd->erf", inputs, w_gate, preferred_element_type=jnp.float32)
    up_pre = jnp.einsum("erd,efd->erf", inputs, w_up, preferred_element_type=jnp.float32)
    active, slopes = silu_pair(gate_pre)
    hidden = (active * up_pre).astype(jnp.bfloat16)
    partial_value = jnp.einsum("erf,efd->erd", hidden, w_down, preferred_element_type=jnp.float32)
    mixed_out = jnp.dot(
        blending, from_experts(partial_value).astype(jnp.float32), precision=lax.Precision.HIGHEST
    ).astype(jnp.bfloat16)
    grad_rows = to_experts(cotangent, place_weighted)
    hidden_grad = jnp.einsum("erd,efd->erf", grad_rows, w_down, preferred_element_type=jnp.float32)
    down_grad = jnp.einsum(
        "erf,erd->efd", hidden, grad_rows, preferred_element_type=jnp.float32
    ).astype(jnp.bfloat16)
    gate_delta = (hidden_grad * up_pre * slopes).astype(jnp.bfloat16)
    up_delta = (hidden_grad * active).astype(jnp.bfloat16)
    gate_grad = jnp.einsum(
        "erf,erd->efd", gate_delta, inputs, preferred_element_type=jnp.float32
    ).astype(jnp.bfloat16)
    up_grad = jnp.einsum(
        "erf,erd->efd", up_delta, inputs, preferred_element_type=jnp.float32
    ).astype(jnp.bfloat16)
    back_rows = jnp.einsum("erf,efd->erd", gate_delta, w_gate, preferred_element_type=jnp.float32)
    back_rows = back_rows + jnp.einsum(
        "erf,efd->erd", up_delta, w_up, preferred_element_type=jnp.float32
    )
    token_grad = jnp.dot(
        blending, from_experts(back_rows).astype(jnp.float32), precision=lax.Precision.HIGHEST
    ).astype(jnp.bfloat16)
    return (mixed_out, token_grad, gate_grad, up_grad, down_grad)


def solution(mesh):
    placed = (
        P("expert", "tensor"),
        P("expert", None),
        P("expert", None),
        P("expert", "tensor"),
        P("expert", "tensor", None),
        P("expert", "tensor", None),
        P("expert", "tensor", None),
    )
    return jax.shard_map(
        shards,
        mesh=mesh,
        in_specs=placed,
        out_specs=(
            P("expert", "tensor"),
            P("expert", "tensor"),
            P("expert", "tensor", None),
            P("expert", "tensor", None),
            P("expert", "tensor", None),
        ),
        check_vma=False,
    )
```

profile of v0, /device:TPU:1, one launch (start us, length us, event | category | flops | bytes accessed | tf_op | source)
XLA Modules:
  0.0 753.1 jit_solution(2396711598475078155)
XLA Ops:
  7.2 0.0 copy-start
  7.2 0.8 copy.33
  8.0 0.1 eq.35
  8.1 0.8 copy.37
  8.9 0.6 reduce-window.6
  9.5 0.2 slice_reduce_fusion
  9.7 0.1 bitcast_bitcast_fusion
  9.8 0.1 reduce_sum.30
  9.9 19.9 %all_gather.6 = bf16[24,4096]{1,0:T(8,128)(2,1)S(1)} all-gather(bf16[24,256]{1,0:T(8,128)(2,1)} %param.7), channel_id=1, replica_groups=mesh['expert'=64,'tensor'=16] {'tensor'}, dimensions={1}, use_global_device_ids=true | all-gather | bytes 208896 | tf_op jit(solution)/shard_map/all_gather | solution.py:37
  29.8 0.2 convert_reduce_fusion
  30.0 0.7 convolution_convert_fusion.2
  30.8 2.2 reshape.129
  33.0 0.0 copy-start.4
  33.0 34.8 %all-to-all-start = ((bf16[64,4,4096]{2,1,0:T(4,128)(2,1)}), bf16[64,4,4096]{2,1,0:T(4,128)(2,1)S(1)}, u32[]{:S(2)}, u32[]{:S(2)}) async-start(bf16[64,4,4096]{2,1,0:T(4,128)(2,1)} %reshape.129), calls=%async_computation | async-start | bytes 4194304 | tf_op jit(solution)/shard_map/all_to_all | solution.py:39
  67.8 0.0 copy-done.4
  67.8 19.1 %all_gather.7 = bf16[24,4096]{1,0:T(8,128)(2,1)S(1)} all-gather(bf16[24,256]{1,0:T(8,128)(2,1)S(1)} %copy-done.4), channel_id=1, replica_groups=mesh['expert'=64,'tensor'=16] {'tensor'}, dimensions={1}, use_global_device_ids=true | all-gather | bytes 208896 | tf_op jit(solution)/shard_map/all_gather | solution.py:37
  86.9 3.2 convolution_convert_fusion
  90.1 4.1 reshape.135
  94.2 171.3 %all-to-all-done = bf16[64,4,4096]{2,1,0:T(4,128)(2,1)S(1)} async-done(((bf16[64,4,4096]{2,1,0:T(4,128)(2,1)}), bf16[64,4,4096]{2,1,0:T(4,128)(2,1)S(1)}, u32[]{:S(2)}, u32[]{:S(2)}) %all-to-all-start) | async-done | bytes 2097184 | tf_op jit(solution)/shard_map/all_to_all | solution.py:39
  265.6 0.0 copy-start.1
  265.6 8.2 %all-to-all-start.2 = ((bf16[64,4,4096]{2,1,0:T(4,128)(2,1)}), bf16[64,4,4096]{2,1,0:T(4,128)(2,1)}, u32[]{:S(2)}, u32[]{:S(2)}) async-start(bf16[64,4,4096]{2,1,0:T(4,128)(2,1)} %reshape.135), calls=%async_computation.3 | async-start | bytes 4194304 | tf_op jit(solution)/shard_map/all_to_all | solution.py:39
  273.8 0.0 copy-done.1
  273.8 0.0 copy-start.3
  273.8 0.0 reduce-scatter.3.cloned.1.call-start
  273.9 2.6 reshape.130
  276.5 0.0 copy-done.3
  276.5 0.0 copy-start.2
  276.5 0.7 fusion.10
  277.2 0.2 copy-done.2
  277.5 0.7 fusion.14
  278.2 192.5 %all-to-all-done.2 = bf16[64,4,4096]{2,1,0:T(4,128)(2,1)} async-done(((bf16[64,4,4096]{2,1,0:T(4,128)(2,1)}), bf16[64,4,4096]{2,1,0:T(4,128)(2,1)}, u32[]{:S(2)}, u32[]{:S(2)}) %all-to-all-start.2) | async-done | bytes 2097184 | tf_op jit(solution)/shard_map/all_to_all | solution.py:39
  470.7 4.0 reshape.136
  474.7 0.0 copy-done
  474.7 2.3 multiply_convert_fusion
  477.0 2.0 fusion.1
  479.1 0.0 reduce-scatter.3.cloned.1.call-update
  479.1 0.0 reduce-scatter.5.cloned.1.call-start
  479.1 0.7 fusion.12
  479.9 2.1 fusion.2
  481.9 0.0 reduce-scatter.5.cloned.1.call-update
  481.9 88.0 %reduce-scatter.3.cloned.1.call-done = bf16[1,256,256]{2,1,0:T(8,128)(2,1)} async-done(((bf16[1,256,4096]{2,1,0:T(8,128)(2,1)}), bf16[1,256,256]{2,1,0:T(8,128)(2,1)}) %reduce-scatter.3.cloned.1.call-update) | async-done | bytes 131088 | tf_op jit(solution)/shard_map/reduce_scatter | solution.py:42
  570.0 1.1 copy.57
  571.1 0.5 broadcast.35
  571.6 1.4 reduce.2
  573.0 0.7 reshape.140
  573.8 25.5 %all-to-all-start.1 = ((bf16[64,2,512]{2,1,0:T(2,128)(2,1)}), bf16[64,2,512]{2,1,0:T(2,128)(2,1)S(1)}, u32[]{:S(2)}, u32[]{:S(2)}) async-start(bf16[64,2,512]{2,1,0:T(2,128)(2,1)} %reshape.140), calls=%async_computation.2 | async-start | bytes 262144 | tf_op jit(solution)/shard_map/all_to_all | solution.py:45
  599.2 86.8 %reduce-scatter.5.cloned.1.call-done = bf16[1,256,256]{2,1,0:T(8,128)(2,1)} async-done(((bf16[1,256,4096]{2,1,0:T(8,128)(2,1)}), bf16[1,256,256]{2,1,0:T(8,128)(2,1)}) %reduce-scatter.5.cloned.1.call-update) | async-done | bytes 131088 | tf_op jit(solution)/shard_map/reduce_scatter | solution.py:42
  686.0 1.1 copy.56
  687.1 1.4 reduce.3
  688.5 0.7 reshape.142
  689.2 0.0 all-to-all-done.1
  689.2 25.4 %all-to-all-start.3 = ((bf16[64,2,512]{2,1,0:T(2,128)(2,1)}), bf16[64,2,512]{2,1,0:T(2,128)(2,1)S(1)}, u32[]{:S(2)}, u32[]{:S(2)}) async-start(bf16[64,2,512]{2,1,0:T(2,128)(2,1)} %reshape.142), calls=%async_computation.5 | async-start | bytes 262144 | tf_op jit(solution)/shard_map/all_to_all | solution.py:45
  714.7 2.8 fusion.5
  717.5 1.2 fusion.4
  718.7 1.2 fusion.3
  720.0 0.1 reshape.141
  720.1 0.8 convolution_convert_fusion.7
  720.9 24.5 %all-to-all-done.3 = bf16[64,2,512]{2,1,0:T(2,128)(2,1)S(1)} async-done(((bf16[64,2,512]{2,1,0:T(2,128)(2,1)}), bf16[64,2,512]{2,1,0:T(2,128)(2,1)S(1)}, u32[]{:S(2)}, u32[]{:S(2)}) %all-to-all-start.3) | async-done | bytes 131104 | tf_op jit(solution)/shard_map/all_to_all | solution.py:45
  745.4 0.1 reshape.143
  745.5 0.8 convolution_convert_fusion.6
  (6 shorter events, 0.1 us)
Async XLA Ops:
  7.2 467.5 %copy-start = (bf16[1,48,4096]{2,1,0:T(8,128)(2,1)S(1)}, bf16[1,48,4096]{2,1,0:T(8,128)(2,1)}, u32[]{:S(2)}) copy-start(bf16[1,48,4096]{2,1,0:T(8,128)(2,1)} %param.13) | copy-start | bytes 1179652
  33.0 34.8 %copy-start.4 = (bf16[24,256]{1,0:T(8,128)(2,1)S(1)}, bf16[24,256]{1,0:T(8,128)(2,1)}, u32[]{:S(2)}) copy-start(bf16[24,256]{1,0:T(8,128)(2,1)} %param.10) | copy-start | bytes 36868
  33.0 232.5 %all-to-all-start = ((bf16[64,4,4096]{2,1,0:T(4,128)(2,1)}), bf16[64,4,4096]{2,1,0:T(4,128)(2,1)S(1)}, u32[]{:S(2)}, u32[]{:S(2)}) async-start(bf16[64,4,4096]{2,1,0:T(4,128)(2,1)} %reshape.129), calls=%async_computation | async-start | bytes 4194304 | tf_op jit(solution)/shard_map/all_to_all | solution.py:39
  265.6 8.2 %copy-start.1 = (bf16[64,4,4096]{2,1,0:T(4,128)(2,1)}, bf16[64,4,4096]{2,1,0:T(4,128)(2,1)S(1)}, u32[]{:S(2)}) copy-start(bf16[64,4,4096]{2,1,0:T(4,128)(2,1)S(1)} %all-to-all-done) | copy-start | bytes 6291460
  265.6 205.2 %all-to-all-start.2 = ((bf16[64,4,4096]{2,1,0:T(4,128)(2,1)}), bf16[64,4,4096]{2,1,0:T(4,128)(2,1)}, u32[]{:S(2)}, u32[]{:S(2)}) async-start(bf16[64,4,4096]{2,1,0:T(4,128)(2,1)} %reshape.135), calls=%async_computation.3 | async-start | bytes 4194304 | tf_op jit(solution)/shard_map/all_to_all | solution.py:39
  273.8 2.7 copy-start.3
  273.8 296.2 %reduce-scatter.3.cloned.1.call-start = ((), (), s32[]{:S(2)}) async-start(), calls=%async_computation.6 | async-start | bytes 2228224 | tf_op jit(solution)/shard_map/reduce_scatter | solution.py:42
  276.5 1.0 copy-start.2
  479.1 206.9 %reduce-scatter.5.cloned.1.call-start = ((), (), s32[]{:S(2)}) async-start(), calls=%async_computation.7 | async-start | bytes 2228224 | tf_op jit(solution)/shard_map/reduce_scatter | solution.py:42
  573.8 115.5 %all-to-all-start.1 = ((bf16[64,2,512]{2,1,0:T(2,128)(2,1)}), bf16[64,2,512]{2,1,0:T(2,128)(2,1)S(1)}, u32[]{:S(2)}, u32[]{:S(2)}) async-start(bf16[64,2,512]{2,1,0:T(2,128)(2,1)} %reshape.140), calls=%async_computation.2 | async-start | bytes 262144 | tf_op jit(solution)/shard_map/all_to_all | solution.py:45
  689.2 56.1 %all-to-all-start.3 = ((bf16[64,2,512]{2,1,0:T(2,128)(2,1)}), bf16[64,2,512]{2,1,0:T(2,128)(2,1)S(1)}, u32[]{:S(2)}, u32[]{:S(2)}) async-start(bf16[64,2,512]{2,1,0:T(2,128)(2,1)} %reshape.142), calls=%async_computation.5 | async-start | bytes 262144 | tf_op jit(solution)/shard_map/all_to_all | solution.py:45
Sparse Core Ops, SparseCore 0:
  479.2 90.7 reduce-scatter.2
  576.1 109.7 reduce-scatter.4
where the time goes:
time: 754 us; the launch traced here: 753 us
  waiting for transfers between devices  563 us (75%)
  starting transfers between devices  94 us (12%)
  blocking collectives  39 us (5%)
  local copies, waits for them, and re-layouts  19.5 us (3%)
  matrix products  19.4 us (3%)
  between operations  14.2 us (2%)
    all_to_all x2, waiting for transfers between devices, to_experts(): lax.all_to_all(buffer, 'expert', split_axis=0, concat_axis=1, tiled=True)  364 us
    reduce_scatter x2, waiting for transfers between devices, from_experts(): lax.psum_scatter(partial_value.astype(jnp.bfloat16), 'tensor', scatter_di...  175 us
    all_to_all x2, starting transfers between devices, from_experts(): lax.all_to_all(summed, 'expert', split_axis=1, concat_axis=0, tiled=True)  50.9 us
    all_to_all x2, starting transfers between devices, to_experts(): lax.all_to_all(buffer, 'expert', split_axis=0, concat_axis=1, tiled=True)  43 us
    all_gather x2, blocking collectives, to_experts(): complete = lax.all_gather(source, 'tensor', axis=1, tiled=True)  39 us
    all_to_all x2, waiting for transfers between devices, from_experts(): lax.all_to_all(summed, 'expert', split_axis=1, concat_axis=0, tiled=True)  24.5 us
  transfers between devices with their start and end apart: 6, of which 5 were waited for; matrix products, arithmetic and copies ran while one was open for 4% of the time, Pallas kernels for 0%

commit v1 on v0

v1 whole, which is shorter than its diff:
```python
import jax
import jax.numpy as jnp
from jax import lax
from jax.sharding import PartitionSpec as P

CAP = 4
F32, BF16 = jnp.float32, jnp.bfloat16


def exchange(values, axis):
    return lax.all_to_all(values, axis, split_axis=0, concat_axis=0, tiled=True)


def slot_weights(routes, gates, experts):
    count = routes.shape[0]
    column = lax.broadcasted_iota(jnp.int32, (1, 1, experts * 2 * CAP), 2)
    chosen = routes[:, :, None] == column // (2 * CAP)
    named = jnp.sum(chosen.astype(F32), axis=1)
    weight = jnp.sum(jnp.where(chosen, gates[:, :, None], 0.0), axis=1)
    row = lax.broadcasted_iota(jnp.int32, (count, count), 0)
    before = (lax.broadcasted_iota(jnp.int32, (count, count), 1) < row).astype(BF16)
    position = jnp.dot(before, named.astype(BF16), preferred_element_type=F32).astype(jnp.int32)
    place = column[0] % (2 * CAP)
    first = named * (position == place)
    second = named * (position + CAP == place) * weight
    return jnp.concatenate([first, second]), jnp.concatenate([first * weight, second])


def shards(tokens, routes, gates, cotangent, w_gate, w_up, w_down):
    experts, groups = lax.axis_size("expert"), lax.axis_size("tensor")
    count, width = tokens.shape
    hidden_units = w_gate.shape[1]
    rows = experts * CAP

    weights = jnp.concatenate([w_gate[0], w_up[0], w_down[0]]).reshape(3 * hidden_units, groups, width)
    weights = exchange(weights.transpose(1, 0, 2), "tensor")
    weights_in, weights_out = weights[:, : 2 * hidden_units], weights[:, 2 * hidden_units :]

    spread, blend = slot_weights(routes, gates, experts)
    sent = lax.dot_general(
        spread,
        jnp.concatenate([tokens, cotangent]).astype(F32),
        (((0,), (0,)), ((), ())),
        precision=lax.Precision.HIGHEST,
    ).astype(BF16)
    arrived = exchange(sent.reshape(experts, 2 * CAP, width), "expert")
    inputs = arrived[:, :CAP].reshape(rows, width)
    grad_rows = arrived[:, CAP:].reshape(rows, width)

    def product(a, b, pattern):
        return jnp.einsum(pattern, a, b, preferred_element_type=F32)

    partial = jnp.concatenate(
        [
            product(weights_in, inputs, "sfd,rd->sfr").astype(BF16),
            product(weights_out, grad_rows, "sfd,rd->sfr").astype(BF16),
        ],
        axis=1,
    )
    summed = jnp.sum(exchange(partial, "tensor").astype(F32), axis=0)
    gate_pre = summed[:hidden_units]
    up_pre = summed[hidden_units : 2 * hidden_units]
    hidden_grad = summed[2 * hidden_units :]
    sigmoid = jax.nn.sigmoid(gate_pre)
    active = gate_pre * sigmoid
    slope = sigmoid * (1.0 + gate_pre * (1.0 - sigmoid))
    mine = jnp.concatenate([hidden_grad * up_pre * slope, hidden_grad * active, active * up_pre]).astype(BF16)
    copies = lax.optimization_barrier(jnp.broadcast_to(mine[None], (groups,) + mine.shape))
    whole = exchange(copies, "tensor")
    deltas, hidden = whole[:, : 2 * hidden_units], whole[:, 2 * hidden_units :]

    expert_out = product(hidden, weights_out, "sfr,sfd->rd").astype(BF16)
    expert_back = product(deltas, weights_in, "sfr,sfd->rd").astype(BF16)
    returned = jnp.concatenate(
        [expert_out.reshape(experts, CAP, width), expert_back.reshape(experts, CAP, width)], axis=1
    )
    returned = exchange(returned, "expert").reshape(2 * rows, width)

    grads = jnp.concatenate(
        [
            product(deltas, inputs, "sfr,rd->sfd").astype(BF16),
            product(hidden, grad_rows, "sfr,rd->sfd").astype(BF16),
        ],
        axis=1,
    )
    grads = exchange(grads, "tensor").transpose(1, 0, 2).reshape(3 * hidden_units, groups * width)

    mixed = jnp.dot(blend, returned.astype(F32), precision=lax.Precision.HIGHEST).astype(BF16)
    return (
        mixed[:count],
        mixed[count:],
        grads[None, :hidden_units],
        grads[None, hidden_units : 2 * hidden_units],
        grads[None, 2 * hidden_units :],
    )


def solution(mesh):
    by_row, by_hidden = P("expert", "tensor"), P("expert", "tensor", None)
    return jax.shard_map(
        shards,
        mesh=mesh,
        in_specs=(by_row, P("expert", None), P("expert", None), by_row, by_hidden, by_hidden, by_hidden),
        out_specs=(by_row, by_row, by_hidden, by_hidden, by_hidden),
        check_vma=False,
    )
```

time: 754 us -> 219 us (0.29)
  waiting for transfers between devices: 563 us -> 101 us
  starting transfers between devices: 94 us -> 55.8 us
  between operations: 14.2 us -> 0.94 us
  matrix products: 19.4 us -> 6.26 us
  local copies, waits for them, and re-layouts: 19.5 us -> 10.1 us
    all_to_all x4, waiting for transfers between devices: 388 us -> 101 us  [exchange(): return lax.all_to_all(values, axis, split_axis=0, concat_axis=0, tiled=True)]
    reduce_scatter x2 -> x0, waiting for transfers between devices: 175 us -> none  [from_experts(): lax.psum_scatter(partial_value.astype(jnp.bfloat16), 'tensor', scatter_di...]
    all_to_all x0 -> x2, blocking collectives: none -> 39.6 us  [exchange(): return lax.all_to_all(values, axis, split_axis=0, concat_axis=0, tiled=True)]
    all_gather x2 -> x0, blocking collectives: 39 us -> none  [to_experts(): complete = lax.all_gather(source, 'tensor', axis=1, tiled=True)]
    all_to_all x4, starting transfers between devices: 93.9 us -> 55.8 us  [exchange(): return lax.all_to_all(values, axis, split_axis=0, concat_axis=0, tiled=True)]
    dot_general x13 -> x9, matrix products: 19.4 us -> 6.26 us  [the longest x6 3.34 us: product(): return jnp.einsum(pattern, a, b, preferred_element_type=F32)]
  transfers between devices with their start and end apart: 6 -> 4, of which waited for: 5 -> 4; matrix products, arithmetic and copies ran while one was open for 4% -> 5% of each run, Pallas kernels for 0% -> 0%
where the time goes in v1:
time: 219 us
  waiting for transfers between devices  101 us (46%)
  starting transfers between devices  55.8 us (25%)
  blocking collectives  39.6 us (18%)
  local copies, waits for them, and re-layouts  10.1 us (5%)
  matrix products  6.26 us (3%)
  other arithmetic  4.53 us (2%)
    all_to_all x4, waiting for transfers between devices, exchange(): return lax.all_to_all(values, axis, split_axis=0, concat_axis=0, tiled=True)  101 us
    all_to_all x4, starting transfers between devices, exchange(): return lax.all_to_all(values, axis, split_axis=0, concat_axis=0, tiled=True)  55.8 us
    all_to_all x2, blocking collectives, exchange(): return lax.all_to_all(values, axis, split_axis=0, concat_axis=0, tiled=True)  39.6 us
  transfers between devices with their start and end apart: 4, of which 4 were waited for; matrix products, arithmetic and copies ran while one was open for 5% of the time, Pallas kernels for 0%

profile of v1, /device:TPU:1, one launch (start us, length us, event | category | flops | bytes accessed | tf_op | source)
XLA Modules:
  0.0 218.5 jit_solution(2047379474802898923)
XLA Ops:
  0.6 0.0 copy-start.6
  0.7 0.8 copy.22
  1.5 0.8 copy.23
  2.2 0.3 fusion.7
  2.5 0.8 fusion.31
  3.3 0.0 copy-start.4
  3.3 0.6 copy-done.4
  3.9 1.9 fusion
  5.8 30.4 %all-to-all-start.1 = ((bf16[64,8,256]{2,1,0:T(8,128)(2,1)}), bf16[64,8,256]{2,1,0:T(8,128)(2,1)S(1)}, u32[]{:S(2)}, u32[]{:S(2)}) async-start(bf16[64,8,256]{2,1,0:T(8,128)(2,1)} %fusion), calls=%async_computation.1 | async-start | bytes 524288 | tf_op jit(solution)/shard_map/all_to_all | solution.py:11
  36.2 0.0 copy-done.6
  36.2 0.1 copy.30
  36.3 0.0 copy-start.8
  36.3 0.1 copy.24
  36.4 0.0 copy-done.7
  36.5 0.1 copy.31
  36.5 0.1 copy.25
  36.7 0.6 copy-done.8
  37.3 0.1 copy.32
  37.4 0.1 copy.26
  37.5 1.1 maximum_bitcast_fusion
  38.6 38.9 %all-to-all-done.1 = bf16[64,8,256]{2,1,0:T(8,128)(2,1)S(1)} async-done(((bf16[64,8,256]{2,1,0:T(8,128)(2,1)}), bf16[64,8,256]{2,1,0:T(8,128)(2,1)S(1)}, u32[]{:S(2)}, u32[]{:S(2)}) %all-to-all-start.1) | async-done | bytes 262176 | tf_op jit(solution)/shard_map/all_to_all | solution.py:11
  77.5 6.8 %all-to-all-start = ((bf16[16,144,256]{2,1,0:T(8,128)(2,1)}), bf16[16,144,256]{2,1,0:T(8,128)(2,1)S(1)}, u32[]{:S(2)}, u32[]{:S(2)}) async-start(bf16[16,144,256]{2,1,0:T(8,128)(2,1)} %maximum_bitcast_fusion), calls=%async_computation | async-start | bytes 2359296 | tf_op jit(solution)/shard_map/all_to_all | solution.py:11
  84.3 0.1 fusion.33
  84.4 0.0 copy-start.2
  84.5 0.0 copy-start
  84.5 15.9 %all-to-all-done = bf16[16,144,256]{2,1,0:T(8,128)(2,1)S(1)} async-done(((bf16[16,144,256]{2,1,0:T(8,128)(2,1)}), bf16[16,144,256]{2,1,0:T(8,128)(2,1)S(1)}, u32[]{:S(2)}, u32[]{:S(2)}) %all-to-all-start) | async-done | bytes 1179680 | tf_op jit(solution)/shard_map/all_to_all | solution.py:11
  100.3 0.3 convolution_convert_fusion.3
  100.6 0.4 convolution_convert_fusion.1
  101.0 0.0 copy-done.2
  101.0 0.0 copy-done
  101.1 0.1 pad_maximum_fusion
  101.1 21.5 %all_to_all.30 = bf16[16,144,256]{2,1,0:T(8,128)(2,1)S(1)} all-to-all(bf16[16,144,256]{2,1,0:T(8,128)(2,1)S(1)} %pad_maximum_fusion), channel_id=1, replica_groups=mesh['expert'=64,'tensor'=16] {'tensor'}, dimensions={0} | all-to-all | bytes 2359296 | tf_op jit(solution)/shard_map/all_to_all | solution.py:11
  122.6 0.2 convert_reduce_fusion
  122.9 0.1 broadcast_in_dim.31
  122.9 0.0 copy-start.1
  123.0 0.0 copy-start.3
  123.0 18.1 %all_to_all.31 = bf16[16,144,256]{2,1,0:T(8,128)(2,1)S(1)} all-to-all(bf16[16,144,256]{2,1,0:T(8,128)(2,1)S(1)} %broadcast_in_dim.31), channel_id=1, replica_groups=mesh['expert'=64,'tensor'=16] {'tensor'}, dimensions={0} | all-to-all | bytes 2359296 | tf_op jit(solution)/shard_map/all_to_all | solution.py:11
  141.0 0.0 copy-done.1
  141.0 0.3 convolution_convert_fusion.2
  141.3 0.0 copy-done.3
  141.3 0.4 convolution_convert_fusion
  141.7 1.1 pad_maximum_fusion.1
  142.8 4.0 %all-to-all-start.5 = ((bf16[16,144,256]{2,1,0:T(8,128)(2,1)}), bf16[16,144,256]{2,1,0:T(8,128)(2,1)S(1)}, u32[]{:S(2)}, u32[]{:S(2)}) async-start(bf16[16,144,256]{2,1,0:T(8,128)(2,1)} %pad_maximum_fusion.1), calls=%async_computation.5 | async-start | bytes 2359296 | tf_op jit(solution)/shard_map/all_to_all | solution.py:11
  146.8 1.0 fusion.2
  147.8 1.6 reshape.121
  149.4 1.1 fusion.1
  150.5 0.9 reshape.122
  151.4 1.7 pad_maximum_fusion.2
  153.1 8.6 %all-to-all-done.5 = bf16[16,144,256]{2,1,0:T(8,128)(2,1)S(1)} async-done(((bf16[16,144,256]{2,1,0:T(8,128)(2,1)}), bf16[16,144,256]{2,1,0:T(8,128)(2,1)S(1)}, u32[]{:S(2)}, u32[]{:S(2)}) %all-to-all-start.5) | async-done | bytes 1179680 | tf_op jit(solution)/shard_map/all_to_all | solution.py:11
  161.7 14.6 %all-to-all-start.4 = ((bf16[64,8,256]{2,1,0:T(8,128)(2,1)}), bf16[64,8,256]{2,1,0:T(8,128)(2,1)S(1)}, u32[]{:S(2)}, u32[]{:S(2)}) async-start(bf16[64,8,256]{2,1,0:T(8,128)(2,1)} %pad_maximum_fusion.2), calls=%async_computation.4 | async-start | bytes 524288 | tf_op jit(solution)/shard_map/all_to_all | solution.py:11
  176.3 0.1 fusion.32
  176.4 0.1 copy.29
  176.6 0.9 broadcast_in_dim.34
  177.5 0.1 copy.28
  177.6 0.0 copy-start.5
  177.6 0.0 copy-start.9
  177.6 0.9 broadcast_in_dim.33
  178.6 0.1 copy.27
  178.7 0.9 broadcast_in_dim.32
  179.6 38.0 %all-to-all-done.4 = bf16[64,8,256]{2,1,0:T(8,128)(2,1)S(1)} async-done(((bf16[64,8,256]{2,1,0:T(8,128)(2,1)}), bf16[64,8,256]{2,1,0:T(8,128)(2,1)S(1)}, u32[]{:S(2)}, u32[]{:S(2)}) %all-to-all-start.4) | async-done | bytes 262176 | tf_op jit(solution)/shard_map/all_to_all | solution.py:11
  217.6 0.0 copy-done.5
  217.6 0.0 copy-done.9
  217.6 0.3 convolution_convert_fusion.6
  217.9 0.6 fusion.34
  (7 shorter events, 0.1 us)
Async XLA Ops:
  0.6 35.6 %copy-start.6 = (bf16[1,48,4096]{2,1,0:T(8,128)(2,1)S(1)}, bf16[1,48,4096]{2,1,0:T(8,128)(2,1)}, u32[]{:S(2)}) copy-start(bf16[1,48,4096]{2,1,0:T(8,128)(2,1)} %param.11) | copy-start | bytes 1179652
  3.3 0.6 copy-start.4
  3.9 32.6 %copy-start.7 = (bf16[1,48,4096]{2,1,0:T(8,128)(2,1)S(1)}, bf16[1,48,4096]{2,1,0:T(8,128)(2,1)}, u32[]{:S(2)}) copy-start(bf16[1,48,4096]{2,1,0:T(8,128)(2,1)} %param.12) | copy-start | bytes 1179652
  5.8 71.7 %all-to-all-start.1 = ((bf16[64,8,256]{2,1,0:T(8,128)(2,1)}), bf16[64,8,256]{2,1,0:T(8,128)(2,1)S(1)}, u32[]{:S(2)}, u32[]{:S(2)}) async-start(bf16[64,8,256]{2,1,0:T(8,128)(2,1)} %fusion), calls=%async_computation.1 | async-start | bytes 524288 | tf_op jit(solution)/shard_map/all_to_all | solution.py:11
  36.3 1.0 copy-start.8
  77.5 22.8 %all-to-all-start = ((bf16[16,144,256]{2,1,0:T(8,128)(2,1)}), bf16[16,144,256]{2,1,0:T(8,128)(2,1)S(1)}, u32[]{:S(2)}, u32[]{:S(2)}) async-start(bf16[16,144,256]{2,1,0:T(8,128)(2,1)} %maximum_bitcast_fusion), calls=%async_computation | async-start | bytes 2359296 | tf_op jit(solution)/shard_map/all_to_all | solution.py:11
  84.4 16.6 %copy-start.2 = (bf16[256,256,1]{1,0,2:T(8,128)(2,1)}, bf16[256,256,1]{1,0,2:T(8,128)(2,1)S(1)}, u32[]{:S(2)}) copy-start(bf16[256,256,1]{1,0,2:T(8,128)(2,1)S(1)} %reshape.124) | copy-start | bytes 393220
  84.5 16.6 %copy-start = (bf16[256,256,1]{1,0,2:T(8,128)(2,1)}, bf16[256,256,1]{1,0,2:T(8,128)(2,1)S(1)}, u32[]{:S(2)}) copy-start(bf16[256,256,1]{1,0,2:T(8,128)(2,1)S(1)} %reshape.125) | copy-start | bytes 393220
  122.9 18.1 %copy-start.1 = (bf16[256,256,1]{1,0,2:T(8,128)(2,1)S(1)}, bf16[256,256,1]{1,0,2:T(8,128)(2,1)}, u32[]{:S(2)}) copy-start(bf16[256,256,1]{1,0,2:T(8,128)(2,1)} %copy-done) | copy-start | bytes 393220
  123.0 18.4 %copy-start.3 = (bf16[256,256,1]{1,0,2:T(8,128)(2,1)S(1)}, bf16[256,256,1]{1,0,2:T(8,128)(2,1)}, u32[]{:S(2)}) copy-start(bf16[256,256,1]{1,0,2:T(8,128)(2,1)} %copy-done.2) | copy-start | bytes 393220
  142.8 18.9 %all-to-all-start.5 = ((bf16[16,144,256]{2,1,0:T(8,128)(2,1)}), bf16[16,144,256]{2,1,0:T(8,128)(2,1)S(1)}, u32[]{:S(2)}, u32[]{:S(2)}) async-start(bf16[16,144,256]{2,1,0:T(8,128)(2,1)} %pad_maximum_fusion.1), calls=%async_computation.5 | async-start | bytes 2359296 | tf_op jit(solution)/shard_map/all_to_all | solution.py:11
  161.7 55.9 %all-to-all-start.4 = ((bf16[64,8,256]{2,1,0:T(8,128)(2,1)}), bf16[64,8,256]{2,1,0:T(8,128)(2,1)S(1)}, u32[]{:S(2)}, u32[]{:S(2)}) async-start(bf16[64,8,256]{2,1,0:T(8,128)(2,1)} %pad_maximum_fusion.2), calls=%async_computation.4 | async-start | bytes 524288 | tf_op jit(solution)/shard_map/all_to_all | solution.py:11
  177.6 40.0 %copy-start.5 = (f32[24,512]{1,0:T(8,128)S(1)}, f32[24,512]{1,0:T(8,128)}, u32[]{:S(2)}) copy-start(f32[24,512]{1,0:T(8,128)} %copy-done.4) | copy-start | bytes 147460
  177.6 40.0 %copy-start.9 = (f32[24,512]{1,0:T(8,128)S(1)}, f32[24,512]{1,0:T(8,128)}, u32[]{:S(2)}) copy-start(f32[24,512]{1,0:T(8,128)} %get-tuple-element.7) | copy-start | bytes 147460

commit v2 on v1

v2 whole, which is shorter than its diff:
```python
import math

import jax
import jax.numpy as jnp
from jax import lax
from jax.sharding import Mesh, PartitionSpec as P

CAP = 4
F32, BF16 = jnp.float32, jnp.bfloat16


def exchange(values, axis):
    return lax.all_to_all(values, axis, split_axis=0, concat_axis=0, tiled=True)


def share(values, axis):
    copies = jnp.broadcast_to(values[None], (lax.axis_size(axis),) + values.shape)
    return exchange(lax.optimization_barrier(copies), axis)


def product(a, b, pattern):
    return jnp.einsum(pattern, a, b, preferred_element_type=F32)


def swap(block_for, axis):
    size, me = lax.axis_size(axis), lax.axis_index(axis)
    moved = [block_for(me)]
    for shift in range(1, size):
        pairs = [(m, (m + shift) % size) for m in range(size)]
        moved.append(lax.ppermute(block_for((me + shift) % size), axis, pairs))
    ordered = []
    for m in range(size):
        shift = (me - m) % size
        block = moved[0]
        for other in range(1, size):
            block = jnp.where(shift == other, moved[other], block)
        ordered.append(block)
    return ordered


def slot_weights(routes, gates, experts):
    count = routes.shape[0]
    column = lax.broadcasted_iota(jnp.int32, (1, 1, experts * 2 * CAP), 2)
    chosen = routes[:, :, None] == column // (2 * CAP)
    named = jnp.sum(chosen.astype(F32), axis=1)
    weight = jnp.sum(jnp.where(chosen, gates[:, :, None], 0.0), axis=1)
    row = lax.broadcasted_iota(jnp.int32, (count, count), 0)
    before = (lax.broadcasted_iota(jnp.int32, (count, count), 1) < row).astype(BF16)
    position = jnp.dot(before, named.astype(BF16), preferred_element_type=F32).astype(jnp.int32)
    place = column[0] % (2 * CAP)
    first = named * (position == place)
    second = named * (position + CAP == place) * weight
    return jnp.concatenate([first, second]), jnp.concatenate([first * weight, second])


def shards(tokens, routes, gates, cotangent, w_gate, w_up, w_down):
    experts, high, wide = lax.axis_size("expert"), lax.axis_size("row"), lax.axis_size("col")
    count, width = tokens.shape
    units = w_gate.shape[1]
    rows = experts * CAP

    spread, blend = slot_weights(routes, gates, experts)
    sent = lax.dot_general(
        spread,
        jnp.concatenate([tokens, cotangent]).astype(F32),
        (((0,), (0,)), ((), ())),
        precision=lax.Precision.HIGHEST,
    ).astype(BF16)
    sent, w_gate, w_up, w_down = lax.optimization_barrier((sent, w_gate, w_up, w_down))
    arrived = exchange(sent.reshape(experts, 2 * CAP, width), "expert")

    weights = jnp.concatenate([w_gate[0], w_up[0], w_down[0]]).reshape(3 * units, high, wide, width)
    weights = jnp.stack(
        swap(lambda m: lax.dynamic_index_in_dim(weights, m, 2, keepdims=False), "col")
    )
    arrived, weights = lax.optimization_barrier((arrived, weights))
    weights_in, weights_out = weights[:, : 2 * units], weights[:, 2 * units :]

    split = jnp.stack([arrived[:, :CAP].reshape(rows, width), arrived[:, CAP:].reshape(rows, width)])
    gathered = share(split, "row")
    inputs, grad_rows = gathered[:, 0], gathered[:, 1]

    partial = jnp.concatenate(
        [
            product(weights_in, inputs, "shyf,yrf->shr").astype(BF16),
            product(weights_out, grad_rows, "shyf,yrf->shr").astype(BF16),
        ],
        axis=1,
    )
    summed = jnp.sum(exchange(partial, "col").astype(F32), axis=0)
    gate_pre, up_pre, hidden_grad = summed[:units], summed[units : 2 * units], summed[2 * units :]
    sigmoid = jax.nn.sigmoid(gate_pre)
    active = gate_pre * sigmoid
    slope = sigmoid * (1.0 + gate_pre * (1.0 - sigmoid))
    mine = jnp.concatenate([hidden_grad * up_pre * slope, hidden_grad * active, active * up_pre]).astype(BF16)
    whole = share(mine, "col")
    deltas, hidden = whole[:, : 2 * units], whole[:, 2 * units :]

    results = jnp.stack(
        [
            product(hidden, weights_out, "shr,shyf->yrf").astype(BF16),
            product(deltas, weights_in, "shr,shyf->yrf").astype(BF16),
        ],
        axis=1,
    )
    results = jnp.sum(exchange(results, "row").astype(F32), axis=0).astype(BF16)
    returned = jnp.concatenate(
        [results[0].reshape(experts, CAP, width), results[1].reshape(experts, CAP, width)], axis=1
    )
    returned, deltas, hidden = lax.optimization_barrier((returned, deltas, hidden))
    returned = exchange(returned, "expert").reshape(2 * rows, width)

    grads = jnp.concatenate(
        [
            product(deltas, inputs, "shr,yrf->shyf").astype(BF16),
            product(hidden, grad_rows, "shr,yrf->shyf").astype(BF16),
        ],
        axis=1,
    )
    grads = jnp.stack(swap(lambda m: lax.dynamic_index_in_dim(grads, m, 0, keepdims=False), "col"), axis=2)
    grads = grads.reshape(3 * units, high * wide * width)
    returned, grads = lax.optimization_barrier((returned, grads))

    mixed = jnp.dot(blend, returned.astype(F32), precision=lax.Precision.HIGHEST).astype(BF16)
    return (
        mixed[:count],
        mixed[count:],
        grads[None, :units],
        grads[None, units : 2 * units],
        grads[None, 2 * units :],
    )


def solution(mesh):
    experts, groups = mesh.devices.shape
    high = max(n for n in range(1, math.isqrt(groups) + 1) if groups % n == 0)
    grid = Mesh(mesh.devices.reshape(experts, high, groups // high), ("expert", "row", "col"))
    by_row, by_hidden = P("expert", ("row", "col")), P("expert", ("row", "col"), None)
    return jax.shard_map(
        shards,
        mesh=grid,
        in_specs=(by_row, P("expert", None), P("expert", None), by_row, by_hidden, by_hidden, by_hidden),
        out_specs=(by_row, by_row, by_hidden, by_hidden, by_hidden),
        check_vma=False,
    )
```

time: 219 us -> 185 us (0.84)
  waiting for transfers between devices: 101 us -> 70.3 us
  starting transfers between devices: 55.8 us -> 63.9 us
  blocking collectives: 39.6 us -> 34.3 us
    all_to_all x4 -> x3, waiting for transfers between devices: 101 us -> 43.1 us  [exchange(): return lax.all_to_all(values, axis, split_axis=0, concat_axis=0, tiled=True)]
    ppermute x0 -> x6, waiting for transfers between devices: none -> 27.2 us  [swap(): moved.append(lax.ppermute(block_for((me + shift) % size), axis, pairs))]
    ppermute x0 -> x6, starting transfers between devices: none -> 17.1 us  [swap(): moved.append(lax.ppermute(block_for((me + shift) % size), axis, pairs))]
    all_to_all x4 -> x3, starting transfers between devices: 55.8 us -> 46.8 us  [exchange(): return lax.all_to_all(values, axis, split_axis=0, concat_axis=0, tiled=True)]
    all_to_all x2 -> x3, blocking collectives: 39.6 us -> 34.3 us  [exchange(): return lax.all_to_all(values, axis, split_axis=0, concat_axis=0, tiled=True)]
  transfers between devices with their start and end apart: 4 -> 9, of which waited for: 4 -> 9; matrix products, arithmetic and copies ran while one was open for 5% -> 2% of each run, Pallas kernels for 0% -> 0%
where the time goes in v2:
time: 185 us
  waiting for transfers between devices  70.3 us (38%)
  starting transfers between devices  63.9 us (35%)
  blocking collectives  34.3 us (19%)
  local copies, waits for them, and re-layouts  7.92 us (4%)
  matrix products  4.43 us (2%)
  other arithmetic  2.39 us (1%)
    all_to_all x3, starting transfers between devices, exchange(): return lax.all_to_all(values, axis, split_axis=0, concat_axis=0, tiled=True)  46.8 us
    all_to_all x3, waiting for transfers between devices, exchange(): return lax.all_to_all(values, axis, split_axis=0, concat_axis=0, tiled=True)  43.1 us
    all_to_all x3, blocking collectives, exchange(): return lax.all_to_all(values, axis, split_axis=0, concat_axis=0, tiled=True)  34.3 us
    ppermute x6, waiting for transfers between devices, swap(): moved.append(lax.ppermute(block_for((me + shift) % size), axis, pairs))  27.2 us
    ppermute x6, starting transfers between devices, swap(): moved.append(lax.ppermute(block_for((me + shift) % size), axis, pairs))  17.1 us
  transfers between devices with their start and end apart: 9, of which 9 were waited for; matrix products, arithmetic and copies ran while one was open for 2% of the time, Pallas kernels for 0%

profile of v2, /device:TPU:1, one launch (start us, length us, event | category | flops | bytes accessed | tf_op | source)
XLA Modules:
  0.0 184.5 jit_solution(2669321446404351747)
XLA Ops:
  0.6 0.0 copy-start.3
  0.6 0.0 copy-start.4
  0.7 0.8 copy.49
  1.5 0.8 copy.50
  2.3 0.3 fusion.8
  2.5 0.1 fusion.55
  2.7 1.9 %convolution_convert_fusion.2 = bf16[512,256]{1,0:T(8,128)(2,1)} fusion(f32[24,512]{1,0:T(8,128)S(1)} %get-tuple-element.53, f32[24,512]{1,0:T(8,128)S(1)} %get-tuple-element.30, bf16[24,256]{1,0:T(8,128)(2,1)} %param.10, bf16[24,256]{1,0:T(8,128)(2,1)} %param.7), kind=kOutput, calls=%fused_computation.16 | convolution fusion | flops 75702272 | bytes 385024 | tf_op jit(solution)/shard_map/dot_general | solution.py:63
  4.6 30.5 %all-to-all-start = ((bf16[64,8,256]{2,1,0:T(8,128)(2,1)}), bf16[64,8,256]{2,1,0:T(8,128)(2,1)S(1)}, u32[]{:S(2)}, u32[]{:S(2)}) async-start(bf16[64,8,256]{2,1,0:T(8,128)(2,1)} %bitcast), calls=%async_computation | async-start | bytes 524288 | tf_op jit(solution)/shard_map/all_to_all | solution.py:13
  35.1 0.0 copy-done.3
  35.1 0.3 concatenate.39
  35.4 0.0 copy-done.4
  35.4 0.3 concatenate.40
  35.7 0.3 concatenate.41
  36.0 0.1 copy_dynamic-update-slice_fusion.2
  36.2 0.1 copy_dynamic-update-slice_fusion.1
  36.3 0.1 copy_dynamic-update-slice_fusion
  36.4 0.1 dynamic-slice_bitcast_fusion
  36.5 4.4 %collective-permute-start = (bf16[144,4,256]{2,0,1:T(8,128)(2,1)S(1)}, bf16[144,4,256]{2,0,1:T(8,128)(2,1)S(1)}, u32[]{:S(2)}, u32[]{:S(2)}) collective-permute-start(bf16[144,4,256]{2,0,1:T(8,128)(2,1)S(1)} %get-tuple-element.48), channel_id=1, source_target_pairs={{0,3},{1,0},{2,1},{3,2},{4,7},{5,4},{6,5},{7,6},{8,11},{9,8},{10,9... | collective-permute-start | bytes 884744 | tf_op jit(solution)/shard_map/ppermute | solution.py:30
  40.9 2.4 %collective-permute-start.1 = (bf16[144,4,256]{2,0,1:T(8,128)(2,1)S(1)}, bf16[144,4,256]{2,0,1:T(8,128)(2,1)S(1)}, u32[]{:S(2)}, u32[]{:S(2)}) collective-permute-start(bf16[144,4,256]{2,0,1:T(8,128)(2,1)S(1)} %get-tuple-element.47), channel_id=1, source_target_pairs={{0,2},{1,3},{2,0},{3,1},{4,6},{5,7},{6,4},{7,5},{8,10},{9,11},{10,... | collective-permute-start | bytes 884744 | tf_op jit(solution)/shard_map/ppermute | solution.py:30
  43.3 2.5 %collective-permute-start.2 = (bf16[144,4,256]{2,0,1:T(8,128)(2,1)S(1)}, bf16[144,4,256]{2,0,1:T(8,128)(2,1)S(1)}, u32[]{:S(2)}, u32[]{:S(2)}) collective-permute-start(bf16[144,4,256]{2,0,1:T(8,128)(2,1)S(1)} %get-tuple-element.46), channel_id=1, source_target_pairs={{0,1},{1,2},{2,3},{3,0},{4,5},{5,6},{6,7},{7,4},{8,9},{9,10},{10,1... | collective-permute-start | bytes 884744 | tf_op jit(solution)/shard_map/ppermute | solution.py:30
  45.9 1.6 collective-permute-done
  47.6 4.6 %collective-permute-done.1 = bf16[144,4,256]{2,0,1:T(8,128)(2,1)S(1)} collective-permute-done((bf16[144,4,256]{2,0,1:T(8,128)(2,1)S(1)}, bf16[144,4,256]{2,0,1:T(8,128)(2,1)S(1)}, u32[]{:S(2)}, u32[]{:S(2)}) %collective-permute-start.1) | collective-permute-done | bytes 294944 | tf_op jit(solution)/shard_map/ppermute | solution.py:30
  52.1 7.4 %collective-permute-done.2 = bf16[144,4,256]{2,0,1:T(8,128)(2,1)S(1)} collective-permute-done((bf16[144,4,256]{2,0,1:T(8,128)(2,1)S(1)}, bf16[144,4,256]{2,0,1:T(8,128)(2,1)S(1)}, u32[]{:S(2)}, u32[]{:S(2)}) %collective-permute-start.2) | collective-permute-done | bytes 294944 | tf_op jit(solution)/shard_map/ppermute | solution.py:30
  59.5 0.1 fusion.22
  59.7 0.2 pad_maximum_fusion
  59.8 16.5 %all-to-all-done = bf16[64,8,256]{2,1,0:T(8,128)(2,1)S(1)} async-done(((bf16[64,8,256]{2,1,0:T(8,128)(2,1)}), bf16[64,8,256]{2,1,0:T(8,128)(2,1)S(1)}, u32[]{:S(2)}, u32[]{:S(2)}) %all-to-all-start) | async-done | bytes 262176 | tf_op jit(solution)/shard_map/all_to_all | solution.py:13
  76.4 0.1 fusion.58
  76.6 0.1 broadcast_in_dim.37
  76.7 16.6 %all_to_all.30 = bf16[4,2,256,256]{3,2,1,0:T(8,128)(2,1)S(1)} all-to-all(bf16[4,2,256,256]{3,2,1,0:T(8,128)(2,1)S(1)} %broadcast_in_dim.37), channel_id=1, replica_groups=mesh['expert'=64,'row'=4,'col'=4] {'row'}, dimensions={0} | all-to-all | bytes 2097152 | tf_op jit(solution)/shard_map/all_to_all | solution.py:13
  93.3 0.4 fusion.4
  93.7 0.3 fusion.5
  94.1 9.7 %all_to_all.31 = bf16[4,144,256]{2,1,0:T(8,128)(2,1)S(1)} all-to-all(bf16[4,144,256]{2,1,0:T(8,128)(2,1)S(1)} %pad_maximum_fusion.3), channel_id=1, replica_groups=mesh['expert'=64,'row'=4,'col'=4] {'col'}, dimensions={0} | all-to-all | bytes 589824 | tf_op jit(solution)/shard_map/all_to_all | solution.py:13
  103.8 8.1 %all_to_all.32 = bf16[4,144,256]{2,1,0:T(8,128)(2,1)S(1)} all-to-all(bf16[4,144,256]{2,1,0:T(8,128)(2,1)S(1)} %broadcast_in_dim.38), channel_id=1, replica_groups=mesh['expert'=64,'row'=4,'col'=4] {'col'}, dimensions={0} | all-to-all | bytes 589824 | tf_op jit(solution)/shard_map/all_to_all | solution.py:13
  111.9 0.3 fusion.2
  112.3 0.5 fusion.3
  112.8 0.1 pad_maximum_fusion.2
  112.9 1.1 copy.56
  113.9 3.5 %all-to-all-start.4 = ((bf16[4,2,256,256]{2,3,1,0:T(8,128)(2,1)}), bf16[4,2,256,256]{2,3,1,0:T(8,128)(2,1)S(1)}, u32[]{:S(2)}, u32[]{:S(2)}) async-start(bf16[4,2,256,256]{2,3,1,0:T(8,128)(2,1)} %copy.56), calls=%async_computation.4 | async-start | bytes 2097152 | tf_op jit(solution)/shard_map/all_to_all | solution.py:13
  117.5 9.7 %all-to-all-done.4 = bf16[4,2,256,256]{2,3,1,0:T(8,128)(2,1)S(1)} async-done(((bf16[4,2,256,256]{2,3,1,0:T(8,128)(2,1)}), bf16[4,2,256,256]{2,3,1,0:T(8,128)(2,1)S(1)}, u32[]{:S(2)}, u32[]{:S(2)}) %all-to-all-start.4) | async-done | bytes 1048608 | tf_op jit(solution)/shard_map/all_to_all | solution.py:13
  127.2 0.3 reduce_sum.42
  127.4 0.0 slice-start.1
  127.4 0.1 copy.58
  127.6 0.1 copy.59
  127.7 0.0 slice-start
  127.8 0.8 pad_maximum_fusion.5
  128.6 12.8 %all-to-all-start.5 = ((bf16[64,8,256]{2,1,0:T(8,128)(2,1)}), bf16[64,8,256]{2,1,0:T(8,128)(2,1)S(1)}, u32[]{:S(2)}, u32[]{:S(2)}) async-start(bf16[64,8,256]{2,1,0:T(8,128)(2,1)} %pad_maximum_fusion.5), calls=%async_computation.5 | async-start | bytes 524288 | tf_op jit(solution)/shard_map/all_to_all | solution.py:13
  141.4 0.3 convolution_convert_fusion.1
  141.7 0.4 convolution_convert_fusion
  142.0 0.1 fusion.19
  142.1 2.8 %collective-permute-start.3 = (bf16[144,4,256]{2,0,1:T(8,128)(2,1)S(1)}, bf16[144,4,256]{2,0,1:T(8,128)(2,1)S(1)}, u32[]{:S(2)}, u32[]{:S(2)}) collective-permute-start(bf16[144,4,256]{2,0,1:T(8,128)(2,1)S(1)} %get-tuple-element.44), channel_id=1, source_target_pairs={{0,3},{1,0},{2,1},{3,2},{4,7},{5,4},{6,5},{7,6},{8,11},{9,8},{10,9... | collective-permute-start | bytes 884744 | tf_op jit(solution)/shard_map/ppermute | solution.py:30
  144.9 3.1 %collective-permute-start.4 = (bf16[144,4,256]{2,0,1:T(8,128)(2,1)S(1)}, bf16[144,4,256]{2,0,1:T(8,128)(2,1)S(1)}, u32[]{:S(2)}, u32[]{:S(2)}) collective-permute-start(bf16[144,4,256]{2,0,1:T(8,128)(2,1)S(1)} %get-tuple-element.45), channel_id=1, source_target_pairs={{0,2},{1,3},{2,0},{3,1},{4,6},{5,7},{6,4},{7,5},{8,10},{9,11},{10,... | collective-permute-start | bytes 884744 | tf_op jit(solution)/shard_map/ppermute | solution.py:30
  148.0 1.9 %collective-permute-start.5 = (bf16[144,4,256]{2,0,1:T(8,128)(2,1)S(1)}, bf16[144,4,256]{2,0,1:T(8,128)(2,1)S(1)}, u32[]{:S(2)}, u32[]{:S(2)}) collective-permute-start(bf16[144,4,256]{2,0,1:T(8,128)(2,1)S(1)} %get-tuple-element.43), channel_id=1, source_target_pairs={{0,1},{1,2},{2,3},{3,0},{4,5},{5,6},{6,7},{7,4},{8,9},{9,10},{10,1... | collective-permute-start | bytes 884744 | tf_op jit(solution)/shard_map/ppermute | solution.py:30
  149.9 2.2 %collective-permute-done.3 = bf16[144,4,256]{2,0,1:T(8,128)(2,1)S(1)} collective-permute-done((bf16[144,4,256]{2,0,1:T(8,128)(2,1)S(1)}, bf16[144,4,256]{2,0,1:T(8,128)(2,1)S(1)}, u32[]{:S(2)}, u32[]{:S(2)}) %collective-permute-start.3) | collective-permute-done | bytes 294944 | tf_op jit(solution)/shard_map/ppermute | solution.py:30
  152.1 4.0 %collective-permute-done.4 = bf16[144,4,256]{2,0,1:T(8,128)(2,1)S(1)} collective-permute-done((bf16[144,4,256]{2,0,1:T(8,128)(2,1)S(1)}, bf16[144,4,256]{2,0,1:T(8,128)(2,1)S(1)}, u32[]{:S(2)}, u32[]{:S(2)}) %collective-permute-start.4) | collective-permute-done | bytes 294944 | tf_op jit(solution)/shard_map/ppermute | solution.py:30
  156.2 7.4 %collective-permute-done.5 = bf16[144,4,256]{2,0,1:T(8,128)(2,1)S(1)} collective-permute-done((bf16[144,4,256]{2,0,1:T(8,128)(2,1)S(1)}, bf16[144,4,256]{2,0,1:T(8,128)(2,1)S(1)}, u32[]{:S(2)}, u32[]{:S(2)}) %collective-permute-start.5) | collective-permute-done | bytes 294944 | tf_op jit(solution)/shard_map/ppermute | solution.py:30
  163.6 0.2 select_bitcast_fusion.3
  163.7 0.1 select_bitcast_fusion.2
  163.8 0.2 pad_maximum_fusion.1
  164.0 0.9 copy.60
  164.9 0.9 reshape.105
  165.8 16.9 %all-to-all-done.5 = bf16[64,8,256]{2,1,0:T(8,128)(2,1)S(1)} async-done(((bf16[64,8,256]{2,1,0:T(8,128)(2,1)}), bf16[64,8,256]{2,1,0:T(8,128)(2,1)S(1)}, u32[]{:S(2)}, u32[]{:S(2)}) %all-to-all-start.5) | async-done | bytes 262176 | tf_op jit(solution)/shard_map/all_to_all | solution.py:13
  182.6 1.0 slice_bitcast_fusion.6
  183.7 0.3 convolution_convert_fusion.4
  183.9 0.6 fusion.59
  (22 shorter events, 0.3 us)
Async XLA Ops:
  0.6 34.5 %copy-start.3 = (bf16[1,48,4096]{2,1,0:T(8,128)(2,1)S(1)}, bf16[1,48,4096]{2,1,0:T(8,128)(2,1)}, u32[]{:S(2)}) copy-start(bf16[1,48,4096]{2,1,0:T(8,128)(2,1)} %param.11) | copy-start | bytes 1179652
  0.6 34.8 %copy-start.4 = (bf16[1,48,4096]{2,1,0:T(8,128)(2,1)S(1)}, bf16[1,48,4096]{2,1,0:T(8,128)(2,1)}, u32[]{:S(2)}) copy-start(bf16[1,48,4096]{2,1,0:T(8,128)(2,1)} %param.12) | copy-start | bytes 1179652
  4.6 31.2 %copy-start.5 = (bf16[1,48,4096]{2,1,0:T(8,128)(2,1)S(1)}, bf16[1,48,4096]{2,1,0:T(8,128)(2,1)}, u32[]{:S(2)}) copy-start(bf16[1,48,4096]{2,1,0:T(8,128)(2,1)} %param.13) | copy-start | bytes 1179652
  4.6 71.8 %all-to-all-start = ((bf16[64,8,256]{2,1,0:T(8,128)(2,1)}), bf16[64,8,256]{2,1,0:T(8,128)(2,1)S(1)}, u32[]{:S(2)}, u32[]{:S(2)}) async-start(bf16[64,8,256]{2,1,0:T(8,128)(2,1)} %bitcast), calls=%async_computation | async-start | bytes 524288 | tf_op jit(solution)/shard_map/all_to_all | solution.py:13
  36.5 11.1 %collective-permute-start = (bf16[144,4,256]{2,0,1:T(8,128)(2,1)S(1)}, bf16[144,4,256]{2,0,1:T(8,128)(2,1)S(1)}, u32[]{:S(2)}, u32[]{:S(2)}) collective-permute-start(bf16[144,4,256]{2,0,1:T(8,128)(2,1)S(1)} %get-tuple-element.48), channel_id=1, source_target_pairs={{0,3},{1,0},{2,1},{3,2},{4,7},{5,4},{6,5},{7,6},{8,11},{9,8},{10,9... | collective-permute-start | bytes 884744 | tf_op jit(solution)/shard_map/ppermute | solution.py:30
  40.9 11.2 %collective-permute-start.1 = (bf16[144,4,256]{2,0,1:T(8,128)(2,1)S(1)}, bf16[144,4,256]{2,0,1:T(8,128)(2,1)S(1)}, u32[]{:S(2)}, u32[]{:S(2)}) collective-permute-start(bf16[144,4,256]{2,0,1:T(8,128)(2,1)S(1)} %get-tuple-element.47), channel_id=1, source_target_pairs={{0,2},{1,3},{2,0},{3,1},{4,6},{5,7},{6,4},{7,5},{8,10},{9,11},{10,... | collective-permute-start | bytes 884744 | tf_op jit(solution)/shard_map/ppermute | solution.py:30
  43.3 16.2 %collective-permute-start.2 = (bf16[144,4,256]{2,0,1:T(8,128)(2,1)S(1)}, bf16[144,4,256]{2,0,1:T(8,128)(2,1)S(1)}, u32[]{:S(2)}, u32[]{:S(2)}) collective-permute-start(bf16[144,4,256]{2,0,1:T(8,128)(2,1)S(1)} %get-tuple-element.46), channel_id=1, source_target_pairs={{0,1},{1,2},{2,3},{3,0},{4,5},{5,6},{6,7},{7,4},{8,9},{9,10},{10,1... | collective-permute-start | bytes 884744 | tf_op jit(solution)/shard_map/ppermute | solution.py:30
  59.8 33.9 %copy-start.1 = (bf16[4,144,4,256]{3,1,2,0:T(8,128)(2,1)}, bf16[4,144,4,256]{3,1,2,0:T(8,128)(2,1)S(1)}, u32[]{:S(2)}) copy-start(bf16[4,144,4,256]{3,1,2,0:T(8,128)(2,1)S(1)} %pad_maximum_fusion) | copy-start | bytes 3538948
  94.1 17.9 %copy-start.2 = (bf16[4,144,4,256]{3,1,2,0:T(8,128)(2,1)S(1)}, bf16[4,144,4,256]{3,1,2,0:T(8,128)(2,1)}, u32[]{:S(2)}) copy-start(bf16[4,144,4,256]{3,1,2,0:T(8,128)(2,1)} %copy-done.1) | copy-start | bytes 3538948
  111.9 5.5 %copy-start = (bf16[4,144,256]{2,1,0:T(8,128)(2,1)}, bf16[4,144,256]{2,1,0:T(8,128)(2,1)S(1)}, u32[]{:S(2)}) copy-start(bf16[4,144,256]{2,1,0:T(8,128)(2,1)S(1)} %all_to_all.32) | copy-start | bytes 884740
  113.9 13.2 %all-to-all-start.4 = ((bf16[4,2,256,256]{2,3,1,0:T(8,128)(2,1)}), bf16[4,2,256,256]{2,3,1,0:T(8,128)(2,1)S(1)}, u32[]{:S(2)}, u32[]{:S(2)}) async-start(bf16[4,2,256,256]{2,3,1,0:T(8,128)(2,1)} %copy.56), calls=%async_computation.4 | async-start | bytes 2097152 | tf_op jit(solution)/shard_map/all_to_all | solution.py:13
  127.4 13.9 %slice-start.1 = ((bf16[4,144,256]{2,1,0:T(8,128)(2,1)}), bf16[4,48,256]{2,1,0:T(8,128)(2,1)S(1)}, s32[]{:S(2)}) async-start(bf16[4,144,256]{2,1,0:T(8,128)(2,1)} %copy-done), calls=%async_computation.7 | async-start | bytes 196608 | tf_op jit(solution)/shard_map/slice | solution.py:97
  127.7 13.9 %slice-start = ((bf16[4,144,256]{2,1,0:T(8,128)(2,1)}), bf16[4,96,256]{2,1,0:T(8,128)(2,1)S(1)}, s32[]{:S(2)}) async-start(bf16[4,144,256]{2,1,0:T(8,128)(2,1)} %copy-done), calls=%async_computation.6 | async-start | bytes 393216 | tf_op jit(solution)/shard_map/slice | solution.py:97
  128.6 54.1 %all-to-all-start.5 = ((bf16[64,8,256]{2,1,0:T(8,128)(2,1)}), bf16[64,8,256]{2,1,0:T(8,128)(2,1)S(1)}, u32[]{:S(2)}, u32[]{:S(2)}) async-start(bf16[64,8,256]{2,1,0:T(8,128)(2,1)} %pad_maximum_fusion.5), calls=%async_computation.5 | async-start | bytes 524288 | tf_op jit(solution)/shard_map/all_to_all | solution.py:13
  142.1 10.0 %collective-permute-start.3 = (bf16[144,4,256]{2,0,1:T(8,128)(2,1)S(1)}, bf16[144,4,256]{2,0,1:T(8,128)(2,1)S(1)}, u32[]{:S(2)}, u32[]{:S(2)}) collective-permute-start(bf16[144,4,256]{2,0,1:T(8,128)(2,1)S(1)} %get-tuple-element.44), channel_id=1, source_target_pairs={{0,3},{1,0},{2,1},{3,2},{4,7},{5,4},{6,5},{7,6},{8,11},{9,8},{10,9... | collective-permute-start | bytes 884744 | tf_op jit(solution)/shard_map/ppermute | solution.py:30
  144.9 11.2 %collective-permute-start.4 = (bf16[144,4,256]{2,0,1:T(8,128)(2,1)S(1)}, bf16[144,4,256]{2,0,1:T(8,128)(2,1)S(1)}, u32[]{:S(2)}, u32[]{:S(2)}) collective-permute-start(bf16[144,4,256]{2,0,1:T(8,128)(2,1)S(1)} %get-tuple-element.45), channel_id=1, source_target_pairs={{0,2},{1,3},{2,0},{3,1},{4,6},{5,7},{6,4},{7,5},{8,10},{9,11},{10,... | collective-permute-start | bytes 884744 | tf_op jit(solution)/shard_map/ppermute | solution.py:30
  148.0 15.5 %collective-permute-start.5 = (bf16[144,4,256]{2,0,1:T(8,128)(2,1)S(1)}, bf16[144,4,256]{2,0,1:T(8,128)(2,1)S(1)}, u32[]{:S(2)}, u32[]{:S(2)}) collective-permute-start(bf16[144,4,256]{2,0,1:T(8,128)(2,1)S(1)} %get-tuple-element.43), channel_id=1, source_target_pairs={{0,1},{1,2},{2,3},{3,0},{4,5},{5,6},{6,7},{7,4},{8,9},{9,10},{10,1... | collective-permute-start | bytes 884744 | tf_op jit(solution)/shard_map/ppermute | solution.py:30

commit v3 on v2

--- a/solution.py
+++ b/solution.py
@@ -87,14 +87,13 @@
         ],
         axis=1,
     )
-    summed = jnp.sum(exchange(partial, "col").astype(F32), axis=0)
-    gate_pre, up_pre, hidden_grad = summed[:units], summed[units : 2 * units], summed[2 * units :]
+    summed = jnp.sum(share(partial, "col").astype(F32), axis=0)
+    gate_pre, up_pre, hidden_grad = summed[:, :units], summed[:, units : 2 * units], summed[:, 2 * units :]
     sigmoid = jax.nn.sigmoid(gate_pre)
     active = gate_pre * sigmoid
     slope = sigmoid * (1.0 + gate_pre * (1.0 - sigmoid))
-    mine = jnp.concatenate([hidden_grad * up_pre * slope, hidden_grad * active, active * up_pre]).astype(BF16)
-    whole = share(mine, "col")
-    deltas, hidden = whole[:, : 2 * units], whole[:, 2 * units :]
+    deltas = jnp.concatenate([hidden_grad * up_pre * slope, hidden_grad * active], axis=1).astype(BF16)
+    hidden = (active * up_pre).astype(BF16)
 
     results = jnp.stack(
         [
@@ -118,17 +117,11 @@
         axis=1,
     )
     grads = jnp.stack(swap(lambda m: lax.dynamic_index_in_dim(grads, m, 0, keepdims=False), "col"), axis=2)
-    grads = grads.reshape(3 * units, high * wide * width)
-    returned, grads = lax.optimization_barrier((returned, grads))
+    grads = grads.reshape(3, 1, units, high * wide * width)
+    returned, *grads = lax.optimization_barrier((returned, grads[0], grads[1], grads[2]))
 
     mixed = jnp.dot(blend, returned.astype(F32), precision=lax.Precision.HIGHEST).astype(BF16)
-    return (
-        mixed[:count],
-        mixed[count:],
-        grads[None, :units],
-        grads[None, units : 2 * units],
-        grads[None, 2 * units :],
-    )
+    return (mixed[:count], mixed[count:], *grads)
 
 
 def solution(mesh):

time: 185 us -> 185 us (level)
  waiting for transfers between devices: 70.3 us -> 66.7 us
  starting transfers between devices: 63.9 us -> 67.3 us
    ppermute x6, waiting for transfers between devices: 27.2 us -> 18.1 us  [swap(): moved.append(lax.ppermute(block_for((me + shift) % size), axis, pairs))]
    all_to_all x3, waiting for transfers between devices: 43.1 us -> 48.5 us  [exchange(): return lax.all_to_all(values, axis, split_axis=0, concat_axis=0, tiled=True)]
    squeeze x0 -> x3, local copies, waits for them, and re-layouts: none -> 3.07 us  [the longest x1 1.03 us: shards(): grads[1]]
    all_to_all x3 -> x2, blocking collectives: 34.3 us -> 33.3 us  [exchange(): return lax.all_to_all(values, axis, split_axis=0, concat_axis=0, tiled=True)]
  transfers between devices with their start and end apart: 9 -> 9, of which waited for: 9 -> 9; matrix products, arithmetic and copies ran while one was open for 2% -> 4% of each run, Pallas kernels for 0% -> 0%
where the time goes in v3:
time: 185 us
  starting transfers between devices  67.3 us (36%)
  waiting for transfers between devices  66.7 us (36%)
  blocking collectives  33.3 us (18%)
  local copies, waits for them, and re-layouts  9.22 us (5%)
  matrix products  4.43 us (2%)
  other arithmetic  2.6 us (1%)
    all_to_all x3, waiting for transfers between devices, exchange(): return lax.all_to_all(values, axis, split_axis=0, concat_axis=0, tiled=True)  48.5 us
    all_to_all x3, starting transfers between devices, exchange(): return lax.all_to_all(values, axis, split_axis=0, concat_axis=0, tiled=True)  48.4 us
    all_to_all x2, blocking collectives, exchange(): return lax.all_to_all(values, axis, split_axis=0, concat_axis=0, tiled=True)  33.3 us
    ppermute x6, starting transfers between devices, swap(): moved.append(lax.ppermute(block_for((me + shift) % size), axis, pairs))  19 us
    ppermute x6, waiting for transfers between devices, swap(): moved.append(lax.ppermute(block_for((me + shift) % size), axis, pairs))  18.1 us
  transfers between devices with their start and end apart: 9, of which 9 were waited for; matrix products, arithmetic and copies ran while one was open for 4% of the time, Pallas kernels for 0%

profile of v3, /device:TPU:1, one launch (start us, length us, event | category | flops | bytes accessed | tf_op | source)
XLA Modules:
  0.0 184.6 jit_solution(7367377492557403422)
XLA Ops:
  0.7 0.8 copy.55
  1.5 0.8 copy.56
  2.3 0.3 fusion.8
  2.5 0.1 fusion.53
  2.7 1.9 %convolution_convert_fusion.2 = bf16[512,256]{1,0:T(8,128)(2,1)} fusion(f32[24,512]{1,0:T(8,128)S(1)} %get-tuple-element.60, f32[24,512]{1,0:T(8,128)S(1)} %get-tuple-element.34, bf16[24,256]{1,0:T(8,128)(2,1)} %param.10, bf16[24,256]{1,0:T(8,128)(2,1)} %param.7), kind=kOutput, calls=%fused_computation.17 | convolution fusion | flops 75702272 | bytes 385024 | tf_op jit(solution)/shard_map/dot_general | solution.py:63
  4.6 30.5 %all-to-all-start = ((bf16[64,8,256]{2,1,0:T(8,128)(2,1)}), bf16[64,8,256]{2,1,0:T(8,128)(2,1)S(1)}, u32[]{:S(2)}, u32[]{:S(2)}) async-start(bf16[64,8,256]{2,1,0:T(8,128)(2,1)} %bitcast), calls=%async_computation | async-start | bytes 524288 | tf_op jit(solution)/shard_map/all_to_all | solution.py:13
  35.1 0.3 concatenate.35
  35.4 0.3 concatenate.36
  35.7 0.3 concatenate.37
  36.0 0.1 copy_dynamic-update-slice_fusion.2
  36.2 0.1 copy_dynamic-update-slice_fusion.1
  36.3 0.1 copy_dynamic-update-slice_fusion
  36.4 0.1 dynamic-slice_bitcast_fusion
  36.5 3.1 %collective-permute-start.2 = (bf16[144,4,256]{2,0,1:T(8,128)(2,1)S(1)}, bf16[144,4,256]{2,0,1:T(8,128)(2,1)S(1)}, u32[]{:S(2)}, u32[]{:S(2)}) collective-permute-start(bf16[144,4,256]{2,0,1:T(8,128)(2,1)S(1)} %get-tuple-element.50), channel_id=1, source_target_pairs={{0,1},{1,2},{2,3},{3,0},{4,5},{5,6},{6,7},{7,4},{8,9},{9,10},{10,1... | collective-permute-start | bytes 884744 | tf_op jit(solution)/shard_map/ppermute | solution.py:30
  39.6 4.4 %collective-permute-start.1 = (bf16[144,4,256]{2,0,1:T(8,128)(2,1)S(1)}, bf16[144,4,256]{2,0,1:T(8,128)(2,1)S(1)}, u32[]{:S(2)}, u32[]{:S(2)}) collective-permute-start(bf16[144,4,256]{2,0,1:T(8,128)(2,1)S(1)} %get-tuple-element.51), channel_id=1, source_target_pairs={{0,2},{1,3},{2,0},{3,1},{4,6},{5,7},{6,4},{7,5},{8,10},{9,11},{10,... | collective-permute-start | bytes 884744 | tf_op jit(solution)/shard_map/ppermute | solution.py:30
  44.0 3.1 %collective-permute-start = (bf16[144,4,256]{2,0,1:T(8,128)(2,1)S(1)}, bf16[144,4,256]{2,0,1:T(8,128)(2,1)S(1)}, u32[]{:S(2)}, u32[]{:S(2)}) collective-permute-start(bf16[144,4,256]{2,0,1:T(8,128)(2,1)S(1)} %get-tuple-element.52), channel_id=1, source_target_pairs={{0,3},{1,0},{2,1},{3,2},{4,7},{5,4},{6,5},{7,6},{8,11},{9,8},{10,9... | collective-permute-start | bytes 884744 | tf_op jit(solution)/shard_map/ppermute | solution.py:30
  47.1 0.6 collective-permute-done.2
  47.7 7.3 %collective-permute-done.1 = bf16[144,4,256]{2,0,1:T(8,128)(2,1)S(1)} collective-permute-done((bf16[144,4,256]{2,0,1:T(8,128)(2,1)S(1)}, bf16[144,4,256]{2,0,1:T(8,128)(2,1)S(1)}, u32[]{:S(2)}, u32[]{:S(2)}) %collective-permute-start.1) | collective-permute-done | bytes 294944 | tf_op jit(solution)/shard_map/ppermute | solution.py:30
  55.0 1.3 collective-permute-done
  56.3 0.1 fusion.22
  56.5 0.2 pad_maximum_fusion
  56.6 19.8 %all-to-all-done = bf16[64,8,256]{2,1,0:T(8,128)(2,1)S(1)} async-done(((bf16[64,8,256]{2,1,0:T(8,128)(2,1)}), bf16[64,8,256]{2,1,0:T(8,128)(2,1)S(1)}, u32[]{:S(2)}, u32[]{:S(2)}) %all-to-all-start) | async-done | bytes 262176 | tf_op jit(solution)/shard_map/all_to_all | solution.py:13
  76.4 0.1 fusion.57
  76.6 0.1 broadcast_in_dim.28
  76.7 16.6 %all_to_all.25 = bf16[4,2,256,256]{3,2,1,0:T(8,128)(2,1)S(1)} all-to-all(bf16[4,2,256,256]{3,2,1,0:T(8,128)(2,1)S(1)} %broadcast_in_dim.28), channel_id=1, replica_groups=mesh['expert'=64,'row'=4,'col'=4] {'row'}, dimensions={0} | all-to-all | bytes 2097152 | tf_op jit(solution)/shard_map/all_to_all | solution.py:13
  93.3 0.3 fusion.5
  93.6 0.4 fusion.4
  94.0 0.1 broadcast_in_dim.29
  94.1 16.6 %all_to_all.26 = bf16[4,4,144,256]{3,2,1,0:T(8,128)(2,1)S(1)} all-to-all(bf16[4,4,144,256]{3,2,1,0:T(8,128)(2,1)S(1)} %broadcast_in_dim.29), channel_id=1, replica_groups=mesh['expert'=64,'row'=4,'col'=4] {'col'}, dimensions={0} | all-to-all | bytes 2359296 | tf_op jit(solution)/shard_map/all_to_all | solution.py:13
  110.8 0.2 convert_reduce_fusion
  110.9 0.1 multiply_convert_fusion.2
  111.1 0.3 fusion.2
  111.4 0.5 fusion.3
  111.9 0.1 pad_maximum_fusion.2
  112.0 1.0 copy.62
  113.1 3.5 %all-to-all-start.3 = ((bf16[4,2,256,256]{2,3,1,0:T(8,128)(2,1)}), bf16[4,2,256,256]{2,3,1,0:T(8,128)(2,1)S(1)}, u32[]{:S(2)}, u32[]{:S(2)}) async-start(bf16[4,2,256,256]{2,3,1,0:T(8,128)(2,1)} %copy.62), calls=%async_computation.3 | async-start | bytes 2097152 | tf_op jit(solution)/shard_map/all_to_all | solution.py:13
  116.6 10.1 %all-to-all-done.3 = bf16[4,2,256,256]{2,3,1,0:T(8,128)(2,1)S(1)} async-done(((bf16[4,2,256,256]{2,3,1,0:T(8,128)(2,1)}), bf16[4,2,256,256]{2,3,1,0:T(8,128)(2,1)S(1)}, u32[]{:S(2)}, u32[]{:S(2)}) %all-to-all-start.3) | async-done | bytes 1048608 | tf_op jit(solution)/shard_map/all_to_all | solution.py:13
  126.7 0.3 reduce_sum.42
  127.0 0.1 copy.64
  127.2 0.1 copy.65
  127.3 0.8 pad_maximum_fusion.5
  128.2 14.3 %all-to-all-start.4 = ((bf16[64,8,256]{2,1,0:T(8,128)(2,1)}), bf16[64,8,256]{2,1,0:T(8,128)(2,1)S(1)}, u32[]{:S(2)}, u32[]{:S(2)}) async-start(bf16[64,8,256]{2,1,0:T(8,128)(2,1)} %pad_maximum_fusion.5), calls=%async_computation.4 | async-start | bytes 524288 | tf_op jit(solution)/shard_map/all_to_all | solution.py:13
  142.5 0.3 convolution_convert_fusion.1
  142.8 0.4 convolution_convert_fusion
  143.1 0.1 fusion.19
  143.2 2.2 %collective-permute-start.5 = (bf16[144,4,256]{2,0,1:T(8,128)(2,1)S(1)}, bf16[144,4,256]{2,0,1:T(8,128)(2,1)S(1)}, u32[]{:S(2)}, u32[]{:S(2)}) collective-permute-start(bf16[144,4,256]{2,0,1:T(8,128)(2,1)S(1)} %get-tuple-element.47), channel_id=1, source_target_pairs={{0,1},{1,2},{2,3},{3,0},{4,5},{5,6},{6,7},{7,4},{8,9},{9,10},{10,1... | collective-permute-start | bytes 884744 | tf_op jit(solution)/shard_map/ppermute | solution.py:30
  145.4 4.3 %collective-permute-start.3 = (bf16[144,4,256]{2,0,1:T(8,128)(2,1)S(1)}, bf16[144,4,256]{2,0,1:T(8,128)(2,1)S(1)}, u32[]{:S(2)}, u32[]{:S(2)}) collective-permute-start(bf16[144,4,256]{2,0,1:T(8,128)(2,1)S(1)} %get-tuple-element.48), channel_id=1, source_target_pairs={{0,3},{1,0},{2,1},{3,2},{4,7},{5,4},{6,5},{7,6},{8,11},{9,8},{10,9... | collective-permute-start | bytes 884744 | tf_op jit(solution)/shard_map/ppermute | solution.py:30
  149.7 1.9 %collective-permute-start.4 = (bf16[144,4,256]{2,0,1:T(8,128)(2,1)S(1)}, bf16[144,4,256]{2,0,1:T(8,128)(2,1)S(1)}, u32[]{:S(2)}, u32[]{:S(2)}) collective-permute-start(bf16[144,4,256]{2,0,1:T(8,128)(2,1)S(1)} %get-tuple-element.49), channel_id=1, source_target_pairs={{0,2},{1,3},{2,0},{3,1},{4,6},{5,7},{6,4},{7,5},{8,10},{9,11},{10,... | collective-permute-start | bytes 884744 | tf_op jit(solution)/shard_map/ppermute | solution.py:30
  151.6 2.8 %collective-permute-done.5 = bf16[144,4,256]{2,0,1:T(8,128)(2,1)S(1)} collective-permute-done((bf16[144,4,256]{2,0,1:T(8,128)(2,1)S(1)}, bf16[144,4,256]{2,0,1:T(8,128)(2,1)S(1)}, u32[]{:S(2)}, u32[]{:S(2)}) %collective-permute-start.5) | collective-permute-done | bytes 294944 | tf_op jit(solution)/shard_map/ppermute | solution.py:30
  154.4 1.6 collective-permute-done.3
  156.0 4.6 %collective-permute-done.4 = bf16[144,4,256]{2,0,1:T(8,128)(2,1)S(1)} collective-permute-done((bf16[144,4,256]{2,0,1:T(8,128)(2,1)S(1)}, bf16[144,4,256]{2,0,1:T(8,128)(2,1)S(1)}, u32[]{:S(2)}, u32[]{:S(2)}) %collective-permute-start.4) | collective-permute-done | bytes 294944 | tf_op jit(solution)/shard_map/ppermute | solution.py:30
  160.6 0.2 select_bitcast_fusion.3
  160.8 0.1 select_bitcast_fusion.2
  160.9 0.2 pad_maximum_fusion.1
  161.0 0.1 fusion.55
  161.2 0.3 copy.68
  161.5 1.0 squeeze.56
  162.5 0.3 copy.67
  162.8 1.0 squeeze.55
  163.8 0.3 copy.66
  164.1 1.0 squeeze.54
  165.2 18.6 %all-to-all-done.4 = bf16[64,8,256]{2,1,0:T(8,128)(2,1)S(1)} async-done(((bf16[64,8,256]{2,1,0:T(8,128)(2,1)}), bf16[64,8,256]{2,1,0:T(8,128)(2,1)S(1)}, u32[]{:S(2)}, u32[]{:S(2)}) %all-to-all-start.4) | async-done | bytes 262176 | tf_op jit(solution)/shard_map/all_to_all | solution.py:13
  183.8 0.3 convolution_convert_fusion.4
  184.0 0.6 fusion.58
  (15 shorter events, 0.2 us)
Async XLA Ops:
  0.6 34.8 %copy-start.1 = (bf16[1,48,4096]{2,1,0:T(8,128)(2,1)S(1)}, bf16[1,48,4096]{2,1,0:T(8,128)(2,1)}, u32[]{:S(2)}) copy-start(bf16[1,48,4096]{2,1,0:T(8,128)(2,1)} %param.12) | copy-start | bytes 1179652
  0.6 34.5 %copy-start = (bf16[1,48,4096]{2,1,0:T(8,128)(2,1)S(1)}, bf16[1,48,4096]{2,1,0:T(8,128)(2,1)}, u32[]{:S(2)}) copy-start(bf16[1,48,4096]{2,1,0:T(8,128)(2,1)} %param.11) | copy-start | bytes 1179652
  4.6 31.2 %copy-start.2 = (bf16[1,48,4096]{2,1,0:T(8,128)(2,1)S(1)}, bf16[1,48,4096]{2,1,0:T(8,128)(2,1)}, u32[]{:S(2)}) copy-start(bf16[1,48,4096]{2,1,0:T(8,128)(2,1)} %param.13) | copy-start | bytes 1179652
  4.6 71.8 %all-to-all-start = ((bf16[64,8,256]{2,1,0:T(8,128)(2,1)}), bf16[64,8,256]{2,1,0:T(8,128)(2,1)S(1)}, u32[]{:S(2)}, u32[]{:S(2)}) async-start(bf16[64,8,256]{2,1,0:T(8,128)(2,1)} %bitcast), calls=%async_computation | async-start | bytes 524288 | tf_op jit(solution)/shard_map/all_to_all | solution.py:13
  36.5 11.2 %collective-permute-start.2 = (bf16[144,4,256]{2,0,1:T(8,128)(2,1)S(1)}, bf16[144,4,256]{2,0,1:T(8,128)(2,1)S(1)}, u32[]{:S(2)}, u32[]{:S(2)}) collective-permute-start(bf16[144,4,256]{2,0,1:T(8,128)(2,1)S(1)} %get-tuple-element.50), channel_id=1, source_target_pairs={{0,1},{1,2},{2,3},{3,0},{4,5},{5,6},{6,7},{7,4},{8,9},{9,10},{10,1... | collective-permute-start | bytes 884744 | tf_op jit(solution)/shard_map/ppermute | solution.py:30
  39.6 15.4 %collective-permute-start.1 = (bf16[144,4,256]{2,0,1:T(8,128)(2,1)S(1)}, bf16[144,4,256]{2,0,1:T(8,128)(2,1)S(1)}, u32[]{:S(2)}, u32[]{:S(2)}) collective-permute-start(bf16[144,4,256]{2,0,1:T(8,128)(2,1)S(1)} %get-tuple-element.51), channel_id=1, source_target_pairs={{0,2},{1,3},{2,0},{3,1},{4,6},{5,7},{6,4},{7,5},{8,10},{9,11},{10,... | collective-permute-start | bytes 884744 | tf_op jit(solution)/shard_map/ppermute | solution.py:30
  44.0 12.3 %collective-permute-start = (bf16[144,4,256]{2,0,1:T(8,128)(2,1)S(1)}, bf16[144,4,256]{2,0,1:T(8,128)(2,1)S(1)}, u32[]{:S(2)}, u32[]{:S(2)}) collective-permute-start(bf16[144,4,256]{2,0,1:T(8,128)(2,1)S(1)} %get-tuple-element.52), channel_id=1, source_target_pairs={{0,3},{1,0},{2,1},{3,2},{4,7},{5,4},{6,5},{7,6},{8,11},{9,8},{10,9... | collective-permute-start | bytes 884744 | tf_op jit(solution)/shard_map/ppermute | solution.py:30
  113.1 13.7 %all-to-all-start.3 = ((bf16[4,2,256,256]{2,3,1,0:T(8,128)(2,1)}), bf16[4,2,256,256]{2,3,1,0:T(8,128)(2,1)S(1)}, u32[]{:S(2)}, u32[]{:S(2)}) async-start(bf16[4,2,256,256]{2,3,1,0:T(8,128)(2,1)} %copy.62), calls=%async_computation.3 | async-start | bytes 2097152 | tf_op jit(solution)/shard_map/all_to_all | solution.py:13
  128.2 55.6 %all-to-all-start.4 = ((bf16[64,8,256]{2,1,0:T(8,128)(2,1)}), bf16[64,8,256]{2,1,0:T(8,128)(2,1)S(1)}, u32[]{:S(2)}, u32[]{:S(2)}) async-start(bf16[64,8,256]{2,1,0:T(8,128)(2,1)} %pad_maximum_fusion.5), calls=%async_computation.4 | async-start | bytes 524288 | tf_op jit(solution)/shard_map/all_to_all | solution.py:13
  143.2 11.2 %collective-permute-start.5 = (bf16[144,4,256]{2,0,1:T(8,128)(2,1)S(1)}, bf16[144,4,256]{2,0,1:T(8,128)(2,1)S(1)}, u32[]{:S(2)}, u32[]{:S(2)}) collective-permute-start(bf16[144,4,256]{2,0,1:T(8,128)(2,1)S(1)} %get-tuple-element.47), channel_id=1, source_target_pairs={{0,1},{1,2},{2,3},{3,0},{4,5},{5,6},{6,7},{7,4},{8,9},{9,10},{10,1... | collective-permute-start | bytes 884744 | tf_op jit(solution)/shard_map/ppermute | solution.py:30
  145.4 10.6 %collective-permute-start.3 = (bf16[144,4,256]{2,0,1:T(8,128)(2,1)S(1)}, bf16[144,4,256]{2,0,1:T(8,128)(2,1)S(1)}, u32[]{:S(2)}, u32[]{:S(2)}) collective-permute-start(bf16[144,4,256]{2,0,1:T(8,128)(2,1)S(1)} %get-tuple-element.48), channel_id=1, source_target_pairs={{0,3},{1,0},{2,1},{3,2},{4,7},{5,4},{6,5},{7,6},{8,11},{9,8},{10,9... | collective-permute-start | bytes 884744 | tf_op jit(solution)/shard_map/ppermute | solution.py:30
  149.7 10.9 %collective-permute-start.4 = (bf16[144,4,256]{2,0,1:T(8,128)(2,1)S(1)}, bf16[144,4,256]{2,0,1:T(8,128)(2,1)S(1)}, u32[]{:S(2)}, u32[]{:S(2)}) collective-permute-start(bf16[144,4,256]{2,0,1:T(8,128)(2,1)S(1)} %get-tuple-element.49), channel_id=1, source_target_pairs={{0,2},{1,3},{2,0},{3,1},{4,6},{5,7},{6,4},{7,5},{8,10},{9,11},{10,... | collective-permute-start | bytes 884744 | tf_op jit(solution)/shard_map/ppermute | solution.py:30

commit v4 on v3

--- a/solution.py
+++ b/solution.py
@@ -3,6 +3,8 @@
 import jax
 import jax.numpy as jnp
 from jax import lax
+from jax.experimental import pallas as pl
+from jax.experimental.pallas import tpu as pltpu
 from jax.sharding import Mesh, PartitionSpec as P
 
 CAP = 4
@@ -48,32 +50,70 @@
     before = (lax.broadcasted_iota(jnp.int32, (count, count), 1) < row).astype(BF16)
     position = jnp.dot(before, named.astype(BF16), preferred_element_type=F32).astype(jnp.int32)
     place = column[0] % (2 * CAP)
-    first = named * (position == place)
-    second = named * (position + CAP == place) * weight
-    return jnp.concatenate([first, second]), jnp.concatenate([first * weight, second])
+    return weight * (position == place), weight * (position + CAP == place)
+
+
+def to_slots_kernel(routes_ref, gates_ref, tokens_ref, cotangent_ref, sent_ref):
+    tops, count = routes_ref.shape
+    slots = sent_ref.shape[0]
+    listed, weights = (jnp.concatenate([ref[...]] * 4, axis=1) for ref in (routes_ref, gates_ref))
+    slot = lax.broadcasted_iota(jnp.int32, (slots, 4 * count), 0)
+    column = lax.broadcasted_iota(jnp.int32, (slots, 4 * count), 1)
+    expert, place = slot // (2 * CAP), slot % (2 * CAP)
+    named = jnp.zeros((slots, 4 * count), F32)
+    weight = jnp.zeros((slots, 4 * count), F32)
+    for k in range(tops):
+        chosen = listed[k : k + 1] == expert
+        named = jnp.where(chosen, 1.0, named)
+        weight = jnp.where(chosen, weights[k : k + 1], weight)
+    earlier = lax.broadcasted_iota(jnp.int32, (4 * count, 4 * count), 0)
+    later = lax.broadcasted_iota(jnp.int32, (4 * count, 4 * count), 1)
+    before = ((earlier < later) & (earlier // count == later // count)).astype(F32).astype(BF16)
+    position = jnp.dot(named.astype(BF16), before, preferred_element_type=F32).astype(jnp.int32)
+    section = column // count
+    high = weight.astype(BF16).astype(F32)
+    middle = (weight - high).astype(BF16).astype(F32)
+    low = weight - high - middle
+    part = jnp.where(section == 0, 1.0, jnp.where(section == 1, high, jnp.where(section == 2, middle, low)))
+    wanted = position + jnp.where(section == 0, 0, CAP)
+    spread = jnp.where((named > 0.0) & (wanted == place), part, 0.0).astype(BF16)
+    cotangents = cotangent_ref[...].astype(F32)
+    sources = jnp.concatenate([tokens_ref[...].astype(F32)] + [cotangents] * 3).astype(BF16)
+    sent_ref[...] = jnp.dot(spread, sources, preferred_element_type=F32).astype(BF16)
+
+
+def to_slots(routes, gates, tokens, cotangent, experts):
+    slots, width = experts * 2 * CAP, tokens.shape[1]
+    return pl.pallas_call(
+        to_slots_kernel,
+        out_shape=jax.ShapeDtypeStruct((slots, width), BF16),
+        grid=(1,),
+        in_specs=[pl.BlockSpec(values.shape, lambda i: (0, 0)) for values in (routes.T, gates.T, tokens, cotangent)],
+        out_specs=pl.BlockSpec((slots, width), lambda i: (0, 0)),
+        compiler_params=pltpu.CompilerParams(vmem_limit_bytes=16 * 1024 * 1024),
+        cost_estimate=pl.CostEstimate(flops=8 * slots * width * tokens.shape[0], bytes_accessed=2 * slots * width, transcendentals=0),
+        name="to_slots",
+    )(routes.T, gates.T, tokens, cotangent)
 
 
 def shards(tokens, routes, gates, cotangent, w_gate, w_up, w_down):
     experts, high, wide = lax.axis_size("expert"), lax.axis_size("row"), lax.axis_size("col")
-    count, width = tokens.shape
+    width = tokens.shape[1]
     units = w_gate.shape[1]
     rows = experts * CAP
 
-    spread, blend = slot_weights(routes, gates, experts)
-    sent = lax.dot_general(
-        spread,
-        jnp.concatenate([tokens, cotangent]).astype(F32),
-        (((0,), (0,)), ((), ())),
-        precision=lax.Precision.HIGHEST,
-    ).astype(BF16)
-    sent, w_gate, w_up, w_down = lax.optimization_barrier((sent, w_gate, w_up, w_down))
+    sent = to_slots(routes, gates, tokens, cotangent, experts)
+    sent, w_gate, w_up, w_down, routes, gates = lax.optimization_barrier(
+        (sent, w_gate, w_up, w_down, routes, gates)
+    )
     arrived = exchange(sent.reshape(experts, 2 * CAP, width), "expert")
 
     weights = jnp.concatenate([w_gate[0], w_up[0], w_down[0]]).reshape(3 * units, high, wide, width)
     weights = jnp.stack(
         swap(lambda m: lax.dynamic_index_in_dim(weights, m, 2, keepdims=False), "col")
     )
-    arrived, weights = lax.optimization_barrier((arrived, weights))
+    blend = slot_weights(routes, gates, experts)
+    arrived, weights, blend = lax.optimization_barrier((arrived, weights, blend))
     weights_in, weights_out = weights[:, : 2 * units], weights[:, 2 * units :]
 
     split = jnp.stack([arrived[:, :CAP].reshape(rows, width), arrived[:, CAP:].reshape(rows, width)])
@@ -95,16 +135,17 @@
     deltas = jnp.concatenate([hidden_grad * up_pre * slope, hidden_grad * active], axis=1).astype(BF16)
     hidden = (active * up_pre).astype(BF16)
 
-    results = jnp.stack(
+    blocks = jnp.concatenate(
         [
-            product(hidden, weights_out, "shr,shyf->yrf").astype(BF16),
-            product(deltas, weights_in, "shr,shyf->yrf").astype(BF16),
+            jnp.concatenate([jnp.zeros_like(deltas), hidden], axis=1),
+            jnp.concatenate([deltas, jnp.zeros_like(hidden)], axis=1),
         ],
-        axis=1,
+        axis=2,
     )
+    results = product(blocks, weights, "shr,shyf->yrf").astype(BF16)
     results = jnp.sum(exchange(results, "row").astype(F32), axis=0).astype(BF16)
     returned = jnp.concatenate(
-        [results[0].reshape(experts, CAP, width), results[1].reshape(experts, CAP, width)], axis=1
+        [results[:rows].reshape(experts, CAP, width), results[rows:].reshape(experts, CAP, width)], axis=1
     )
     returned, deltas, hidden = lax.optimization_barrier((returned, deltas, hidden))
     returned = exchange(returned, "expert").reshape(2 * rows, width)
@@ -120,8 +161,9 @@
     grads = grads.reshape(3, 1, units, high * wide * width)
     returned, *grads = lax.optimization_barrier((returned, grads[0], grads[1], grads[2]))
 
-    mixed = jnp.dot(blend, returned.astype(F32), precision=lax.Precision.HIGHEST).astype(BF16)
-    return (mixed[:count], mixed[count:], *grads)
+    returned = returned.astype(F32)
+    mixed, token_grad = (jnp.dot(gate, returned, precision=lax.Precision.HIGHEST).astype(BF16) for gate in blend)
+    return (mixed, token_grad, *grads)
 
 
 def solution(mesh):

time: 185 us -> 184 us (level)
  blocking collectives: 33.3 us -> 46.2 us
  waiting for transfers between devices: 66.7 us -> 55.9 us
  starting transfers between devices: 67.3 us -> 63.4 us
    all_to_all x2 -> x3, blocking collectives: 33.3 us -> 46.2 us  [exchange(): return lax.all_to_all(values, axis, split_axis=0, concat_axis=0, tiled=True)]
    all_to_all x3 -> x2, waiting for transfers between devices: 48.5 us -> 38.4 us  [exchange(): return lax.all_to_all(values, axis, split_axis=0, concat_axis=0, tiled=True)]
    all_to_all x3 -> x2, starting transfers between devices: 48.4 us -> 44.4 us  [exchange(): return lax.all_to_all(values, axis, split_axis=0, concat_axis=0, tiled=True)]
  transfers between devices with their start and end apart: 9 -> 8, of which waited for: 9 -> 7; matrix products, arithmetic and copies ran while one was open for 4% -> 4% of each run, Pallas kernels for 0% -> 0%
where the time goes in v4:
time: 184 us; the launch traced here: 183 us
  starting transfers between devices  63.4 us (34%)
  waiting for transfers between devices  55.9 us (30%)
  blocking collectives  46.2 us (25%)
  local copies, waits for them, and re-layouts  8.92 us (5%)
  matrix products  4.16 us (2%)
  other arithmetic  2.49 us (1%)
    all_to_all x3, blocking collectives, exchange(): return lax.all_to_all(values, axis, split_axis=0, concat_axis=0, tiled=True)  46.2 us
    all_to_all x2, starting transfers between devices, exchange(): return lax.all_to_all(values, axis, split_axis=0, concat_axis=0, tiled=True)  44.4 us
    all_to_all x2, waiting for transfers between devices, exchange(): return lax.all_to_all(values, axis, split_axis=0, concat_axis=0, tiled=True)  38.4 us
    ppermute x6, starting transfers between devices, swap(): moved.append(lax.ppermute(block_for((me + shift) % size), axis, pairs))  19 us
    ppermute x6, waiting for transfers between devices, swap(): moved.append(lax.ppermute(block_for((me + shift) % size), axis, pairs))  17.5 us
  transfers between devices with their start and end apart: 8, of which 7 were waited for; matrix products, arithmetic and copies ran while one was open for 4% of the time, Pallas kernels for 0%

profile of v4, /device:TPU:1, one launch (start us, length us, event | category | flops | bytes accessed | tf_op | source)
XLA Modules:
  0.0 183.5 jit_solution(13631580947628207023)
XLA Ops:
  0.6 0.0 copy-start
  0.6 0.7 copy-done
  1.3 0.7 copy-done.2
  2.0 0.7 copy-done.4
  2.7 0.7 copy-done.5
  3.4 1.3 to_slots.1
  4.8 30.4 %all-to-all-start = ((bf16[64,8,256]{2,1,0:T(8,128)(2,1)}), bf16[64,8,256]{2,1,0:T(8,128)(2,1)S(1)}, u32[]{:S(2)}, u32[]{:S(2)}) async-start(bf16[64,8,256]{2,1,0:T(8,128)(2,1)} %bitcast.2), calls=%async_computation | async-start | bytes 524288 | tf_op jit(solution)/shard_map/all_to_all | solution.py:15
  35.2 0.3 concatenate.32
  35.5 0.3 concatenate.33
  35.8 0.3 concatenate.34
  36.1 0.1 copy_dynamic-update-slice_fusion.2
  36.2 0.1 copy_dynamic-update-slice_fusion.1
  36.4 0.1 copy_dynamic-update-slice_fusion
  36.5 0.1 dynamic-slice_bitcast_fusion
  36.6 3.1 %collective-permute-start.2 = (bf16[144,4,256]{2,0,1:T(8,128)(2,1)S(1)}, bf16[144,4,256]{2,0,1:T(8,128)(2,1)S(1)}, u32[]{:S(2)}, u32[]{:S(2)}) collective-permute-start(bf16[144,4,256]{2,0,1:T(8,128)(2,1)S(1)} %get-tuple-element.56), channel_id=1, source_target_pairs={{0,1},{1,2},{2,3},{3,0},{4,5},{5,6},{6,7},{7,4},{8,9},{9,10},{10,1... | collective-permute-start | bytes 884744 | tf_op jit(solution)/shard_map/ppermute | solution.py:32
  39.7 4.4 %collective-permute-start.1 = (bf16[144,4,256]{2,0,1:T(8,128)(2,1)S(1)}, bf16[144,4,256]{2,0,1:T(8,128)(2,1)S(1)}, u32[]{:S(2)}, u32[]{:S(2)}) collective-permute-start(bf16[144,4,256]{2,0,1:T(8,128)(2,1)S(1)} %get-tuple-element.57), channel_id=1, source_target_pairs={{0,2},{1,3},{2,0},{3,1},{4,6},{5,7},{6,4},{7,5},{8,10},{9,11},{10,... | collective-permute-start | bytes 884744 | tf_op jit(solution)/shard_map/ppermute | solution.py:32
  44.1 3.1 %collective-permute-start = (bf16[144,4,256]{2,0,1:T(8,128)(2,1)S(1)}, bf16[144,4,256]{2,0,1:T(8,128)(2,1)S(1)}, u32[]{:S(2)}, u32[]{:S(2)}) collective-permute-start(bf16[144,4,256]{2,0,1:T(8,128)(2,1)S(1)} %get-tuple-element.58), channel_id=1, source_target_pairs={{0,3},{1,0},{2,1},{3,2},{4,7},{5,4},{6,5},{7,6},{8,11},{9,8},{10,9... | collective-permute-start | bytes 884744 | tf_op jit(solution)/shard_map/ppermute | solution.py:32
  47.2 0.1 copy.52
  47.3 0.1 copy.53
  47.4 0.3 fusion.13
  47.7 0.1 fusion.40
  47.9 7.3 %collective-permute-done.1 = bf16[144,4,256]{2,0,1:T(8,128)(2,1)S(1)} collective-permute-done((bf16[144,4,256]{2,0,1:T(8,128)(2,1)S(1)}, bf16[144,4,256]{2,0,1:T(8,128)(2,1)S(1)}, u32[]{:S(2)}, u32[]{:S(2)}) %collective-permute-start.1) | collective-permute-done | bytes 294944 | tf_op jit(solution)/shard_map/ppermute | solution.py:32
  55.1 1.3 collective-permute-done
  56.4 0.1 fusion.27
  56.6 0.2 pad_maximum_fusion
  56.7 19.7 %all-to-all-done = bf16[64,8,256]{2,1,0:T(8,128)(2,1)S(1)} async-done(((bf16[64,8,256]{2,1,0:T(8,128)(2,1)}), bf16[64,8,256]{2,1,0:T(8,128)(2,1)S(1)}, u32[]{:S(2)}, u32[]{:S(2)}) %all-to-all-start) | async-done | bytes 262176 | tf_op jit(solution)/shard_map/all_to_all | solution.py:15
  76.5 0.1 fusion.55
  76.7 0.1 broadcast_in_dim.18
  76.7 16.6 %all_to_all.25 = bf16[4,2,256,256]{3,2,1,0:T(8,128)(2,1)S(1)} all-to-all(bf16[4,2,256,256]{3,2,1,0:T(8,128)(2,1)S(1)} %broadcast_in_dim.18), channel_id=1, replica_groups=mesh['expert'=64,'row'=4,'col'=4] {'row'}, dimensions={0} | all-to-all | bytes 2097152 | tf_op jit(solution)/shard_map/all_to_all | solution.py:15
  93.3 0.3 fusion.4
  93.7 0.4 fusion.3
  94.1 0.1 broadcast_in_dim.19
  94.2 16.6 %all_to_all.26 = bf16[4,4,144,256]{3,2,1,0:T(8,128)(2,1)S(1)} all-to-all(bf16[4,4,144,256]{3,2,1,0:T(8,128)(2,1)S(1)} %broadcast_in_dim.19), channel_id=1, replica_groups=mesh['expert'=64,'row'=4,'col'=4] {'col'}, dimensions={0} | all-to-all | bytes 2359296 | tf_op jit(solution)/shard_map/all_to_all | solution.py:15
  110.8 0.2 convert_reduce_fusion
  111.0 0.1 multiply_convert_fusion.2
  111.2 1.0 fusion
  112.2 12.9 %all_to_all.27 = bf16[4,512,256]{1,2,0:T(8,128)(2,1)S(1)} all-to-all(bf16[4,512,256]{1,2,0:T(8,128)(2,1)S(1)} %fusion), channel_id=1, replica_groups=mesh['expert'=64,'row'=4,'col'=4] {'row'}, dimensions={0} | all-to-all | bytes 2097152 | tf_op jit(solution)/shard_map/all_to_all | solution.py:15
  125.1 0.2 reduce_sum.42
  125.4 0.1 copy.56
  125.5 0.1 copy.57
  125.7 0.8 pad_maximum_fusion.4
  126.5 14.0 %all-to-all-start.4 = ((bf16[64,8,256]{2,1,0:T(8,128)(2,1)}), bf16[64,8,256]{2,1,0:T(8,128)(2,1)S(1)}, u32[]{:S(2)}, u32[]{:S(2)}) async-start(bf16[64,8,256]{2,1,0:T(8,128)(2,1)} %pad_maximum_fusion.4), calls=%async_computation.4 | async-start | bytes 524288 | tf_op jit(solution)/shard_map/all_to_all | solution.py:15
  140.5 0.3 convolution_convert_fusion.1
  140.8 0.4 convolution_convert_fusion
  141.2 0.1 fusion.23
  141.2 2.2 %collective-permute-start.5 = (bf16[144,4,256]{2,0,1:T(8,128)(2,1)S(1)}, bf16[144,4,256]{2,0,1:T(8,128)(2,1)S(1)}, u32[]{:S(2)}, u32[]{:S(2)}) collective-permute-start(bf16[144,4,256]{2,0,1:T(8,128)(2,1)S(1)} %get-tuple-element.53), channel_id=1, source_target_pairs={{0,1},{1,2},{2,3},{3,0},{4,5},{5,6},{6,7},{7,4},{8,9},{9,10},{10,1... | collective-permute-start | bytes 884744 | tf_op jit(solution)/shard_map/ppermute | solution.py:32
  143.4 4.3 %collective-permute-start.3 = (bf16[144,4,256]{2,0,1:T(8,128)(2,1)S(1)}, bf16[144,4,256]{2,0,1:T(8,128)(2,1)S(1)}, u32[]{:S(2)}, u32[]{:S(2)}) collective-permute-start(bf16[144,4,256]{2,0,1:T(8,128)(2,1)S(1)} %get-tuple-element.54), channel_id=1, source_target_pairs={{0,3},{1,0},{2,1},{3,2},{4,7},{5,4},{6,5},{7,6},{8,11},{9,8},{10,9... | collective-permute-start | bytes 884744 | tf_op jit(solution)/shard_map/ppermute | solution.py:32
  147.7 1.9 %collective-permute-start.4 = (bf16[144,4,256]{2,0,1:T(8,128)(2,1)S(1)}, bf16[144,4,256]{2,0,1:T(8,128)(2,1)S(1)}, u32[]{:S(2)}, u32[]{:S(2)}) collective-permute-start(bf16[144,4,256]{2,0,1:T(8,128)(2,1)S(1)} %get-tuple-element.55), channel_id=1, source_target_pairs={{0,2},{1,3},{2,0},{3,1},{4,6},{5,7},{6,4},{7,5},{8,10},{9,11},{10,... | collective-permute-start | bytes 884744 | tf_op jit(solution)/shard_map/ppermute | solution.py:32
  149.7 2.8 %collective-permute-done.5 = bf16[144,4,256]{2,0,1:T(8,128)(2,1)S(1)} collective-permute-done((bf16[144,4,256]{2,0,1:T(8,128)(2,1)S(1)}, bf16[144,4,256]{2,0,1:T(8,128)(2,1)S(1)}, u32[]{:S(2)}, u32[]{:S(2)}) %collective-permute-start.5) | collective-permute-done | bytes 294944 | tf_op jit(solution)/shard_map/ppermute | solution.py:32
  152.5 1.6 collective-permute-done.3
  154.0 4.6 %collective-permute-done.4 = bf16[144,4,256]{2,0,1:T(8,128)(2,1)S(1)} collective-permute-done((bf16[144,4,256]{2,0,1:T(8,128)(2,1)S(1)}, bf16[144,4,256]{2,0,1:T(8,128)(2,1)S(1)}, u32[]{:S(2)}, u32[]{:S(2)}) %collective-permute-start.4) | collective-permute-done | bytes 294944 | tf_op jit(solution)/shard_map/ppermute | solution.py:32
  158.6 0.2 select_bitcast_fusion.3
  158.8 0.1 select_bitcast_fusion.2
  158.9 0.2 pad_maximum_fusion.1
  159.1 0.1 fusion.53
  159.2 0.3 copy.60
  159.5 1.0 squeeze.56
  160.5 0.3 copy.59
  160.8 1.0 squeeze.55
  161.9 0.3 copy.58
  162.2 1.0 squeeze.54
  163.2 18.6 %all-to-all-done.4 = bf16[64,8,256]{2,1,0:T(8,128)(2,1)S(1)} async-done(((bf16[64,8,256]{2,1,0:T(8,128)(2,1)}), bf16[64,8,256]{2,1,0:T(8,128)(2,1)S(1)}, u32[]{:S(2)}, u32[]{:S(2)}) %all-to-all-start.4) | async-done | bytes 262176 | tf_op jit(solution)/shard_map/all_to_all | solution.py:15
  181.8 0.8 convolution_convert_fusion.3
  182.6 0.8 convolution_convert_fusion.4
  (23 shorter events, 0.3 us)
Async XLA Ops:
  0.6 0.7 copy-start
  1.3 0.7 copy-start.2
  2.0 0.7 copy-start.4
  2.7 0.7 copy-start.5
  3.4 31.8 %copy-start.6 = (bf16[1,48,4096]{2,1,0:T(8,128)(2,1)S(1)}, bf16[1,48,4096]{2,1,0:T(8,128)(2,1)}, u32[]{:S(2)}) copy-start(bf16[1,48,4096]{2,1,0:T(8,128)(2,1)} %param.11) | copy-start | bytes 1179652
  3.4 32.1 %copy-start.7 = (bf16[1,48,4096]{2,1,0:T(8,128)(2,1)S(1)}, bf16[1,48,4096]{2,1,0:T(8,128)(2,1)}, u32[]{:S(2)}) copy-start(bf16[1,48,4096]{2,1,0:T(8,128)(2,1)} %param.12) | copy-start | bytes 1179652
  3.4 32.4 %copy-start.8 = (bf16[1,48,4096]{2,1,0:T(8,128)(2,1)S(1)}, bf16[1,48,4096]{2,1,0:T(8,128)(2,1)}, u32[]{:S(2)}) copy-start(bf16[1,48,4096]{2,1,0:T(8,128)(2,1)} %param.13) | copy-start | bytes 1179652
  4.8 71.7 %all-to-all-start = ((bf16[64,8,256]{2,1,0:T(8,128)(2,1)}), bf16[64,8,256]{2,1,0:T(8,128)(2,1)S(1)}, u32[]{:S(2)}, u32[]{:S(2)}) async-start(bf16[64,8,256]{2,1,0:T(8,128)(2,1)} %bitcast.2), calls=%async_computation | async-start | bytes 524288 | tf_op jit(solution)/shard_map/all_to_all | solution.py:15
  36.4 10.9 %copy-start.1 = (s32[24,8]{0,1:T(8,128)S(1)}, s32[24,8]{0,1:T(8,128)}, u32[]{:S(2)}) copy-start(s32[24,8]{0,1:T(8,128)} %param.8) | copy-start | bytes 2308
  36.4 11.0 %copy-start.3 = (f32[24,8]{0,1:T(8,128)S(1)}, f32[24,8]{0,1:T(8,128)}, u32[]{:S(2)}) copy-start(f32[24,8]{0,1:T(8,128)} %param.9) | copy-start | bytes 2308
  36.6 11.3 %collective-permute-start.2 = (bf16[144,4,256]{2,0,1:T(8,128)(2,1)S(1)}, bf16[144,4,256]{2,0,1:T(8,128)(2,1)S(1)}, u32[]{:S(2)}, u32[]{:S(2)}) collective-permute-start(bf16[144,4,256]{2,0,1:T(8,128)(2,1)S(1)} %get-tuple-element.56), channel_id=1, source_target_pairs={{0,1},{1,2},{2,3},{3,0},{4,5},{5,6},{6,7},{7,4},{8,9},{9,10},{10,1... | collective-permute-start | bytes 884744 | tf_op jit(solution)/shard_map/ppermute | solution.py:32
  39.7 15.4 %collective-permute-start.1 = (bf16[144,4,256]{2,0,1:T(8,128)(2,1)S(1)}, bf16[144,4,256]{2,0,1:T(8,128)(2,1)S(1)}, u32[]{:S(2)}, u32[]{:S(2)}) collective-permute-start(bf16[144,4,256]{2,0,1:T(8,128)(2,1)S(1)} %get-tuple-element.57), channel_id=1, source_target_pairs={{0,2},{1,3},{2,0},{3,1},{4,6},{5,7},{6,4},{7,5},{8,10},{9,11},{10,... | collective-permute-start | bytes 884744 | tf_op jit(solution)/shard_map/ppermute | solution.py:32
  44.1 12.3 %collective-permute-start = (bf16[144,4,256]{2,0,1:T(8,128)(2,1)S(1)}, bf16[144,4,256]{2,0,1:T(8,128)(2,1)S(1)}, u32[]{:S(2)}, u32[]{:S(2)}) collective-permute-start(bf16[144,4,256]{2,0,1:T(8,128)(2,1)S(1)} %get-tuple-element.58), channel_id=1, source_target_pairs={{0,3},{1,0},{2,1},{3,2},{4,7},{5,4},{6,5},{7,6},{8,11},{9,8},{10,9... | collective-permute-start | bytes 884744 | tf_op jit(solution)/shard_map/ppermute | solution.py:32
  126.5 55.3 %all-to-all-start.4 = ((bf16[64,8,256]{2,1,0:T(8,128)(2,1)}), bf16[64,8,256]{2,1,0:T(8,128)(2,1)S(1)}, u32[]{:S(2)}, u32[]{:S(2)}) async-start(bf16[64,8,256]{2,1,0:T(8,128)(2,1)} %pad_maximum_fusion.4), calls=%async_computation.4 | async-start | bytes 524288 | tf_op jit(solution)/shard_map/all_to_all | solution.py:15
  141.2 11.2 %collective-permute-start.5 = (bf16[144,4,256]{2,0,1:T(8,128)(2,1)S(1)}, bf16[144,4,256]{2,0,1:T(8,128)(2,1)S(1)}, u32[]{:S(2)}, u32[]{:S(2)}) collective-permute-start(bf16[144,4,256]{2,0,1:T(8,128)(2,1)S(1)} %get-tuple-element.53), channel_id=1, source_target_pairs={{0,1},{1,2},{2,3},{3,0},{4,5},{5,6},{6,7},{7,4},{8,9},{9,10},{10,1... | collective-permute-start | bytes 884744 | tf_op jit(solution)/shard_map/ppermute | solution.py:32
  143.4 10.6 %collective-permute-start.3 = (bf16[144,4,256]{2,0,1:T(8,128)(2,1)S(1)}, bf16[144,4,256]{2,0,1:T(8,128)(2,1)S(1)}, u32[]{:S(2)}, u32[]{:S(2)}) collective-permute-start(bf16[144,4,256]{2,0,1:T(8,128)(2,1)S(1)} %get-tuple-element.54), channel_id=1, source_target_pairs={{0,3},{1,0},{2,1},{3,2},{4,7},{5,4},{6,5},{7,6},{8,11},{9,8},{10,9... | collective-permute-start | bytes 884744 | tf_op jit(solution)/shard_map/ppermute | solution.py:32
  147.7 10.9 %collective-permute-start.4 = (bf16[144,4,256]{2,0,1:T(8,128)(2,1)S(1)}, bf16[144,4,256]{2,0,1:T(8,128)(2,1)S(1)}, u32[]{:S(2)}, u32[]{:S(2)}) collective-permute-start(bf16[144,4,256]{2,0,1:T(8,128)(2,1)S(1)} %get-tuple-element.55), channel_id=1, source_target_pairs={{0,2},{1,3},{2,0},{3,1},{4,6},{5,7},{6,4},{7,5},{8,10},{9,11},{10,... | collective-permute-start | bytes 884744 | tf_op jit(solution)/shard_map/ppermute | solution.py:32

commit v5 on v4

--- a/solution.py
+++ b/solution.py
@@ -4,7 +4,6 @@
 import jax.numpy as jnp
 from jax import lax
 from jax.experimental import pallas as pl
-from jax.experimental.pallas import tpu as pltpu
 from jax.sharding import Mesh, PartitionSpec as P
 
 CAP = 4
@@ -50,7 +49,7 @@
     before = (lax.broadcasted_iota(jnp.int32, (count, count), 1) < row).astype(BF16)
     position = jnp.dot(before, named.astype(BF16), preferred_element_type=F32).astype(jnp.int32)
     place = column[0] % (2 * CAP)
-    return weight * (position == place), weight * (position + CAP == place)
+    return jnp.concatenate([weight * (position == place), weight * (position + CAP == place)])
 
 
 def to_slots_kernel(routes_ref, gates_ref, tokens_ref, cotangent_ref, sent_ref):
@@ -90,7 +89,6 @@
         grid=(1,),
         in_specs=[pl.BlockSpec(values.shape, lambda i: (0, 0)) for values in (routes.T, gates.T, tokens, cotangent)],
         out_specs=pl.BlockSpec((slots, width), lambda i: (0, 0)),
-        compiler_params=pltpu.CompilerParams(vmem_limit_bytes=16 * 1024 * 1024),
         cost_estimate=pl.CostEstimate(flops=8 * slots * width * tokens.shape[0], bytes_accessed=2 * slots * width, transcendentals=0),
         name="to_slots",
     )(routes.T, gates.T, tokens, cotangent)
@@ -161,9 +159,9 @@
     grads = grads.reshape(3, 1, units, high * wide * width)
     returned, *grads = lax.optimization_barrier((returned, grads[0], grads[1], grads[2]))
 
-    returned = returned.astype(F32)
-    mixed, token_grad = (jnp.dot(gate, returned, precision=lax.Precision.HIGHEST).astype(BF16) for gate in blend)
-    return (mixed, token_grad, *grads)
+    mixed = jnp.dot(blend, returned.astype(F32), precision=lax.Precision.HIGHEST).astype(BF16)
+    count = tokens.shape[0]
+    return (mixed[:count], mixed[count:], *grads)
 
 
 def solution(mesh):

time: 184 us -> 181 us (0.984)
  local copies, waits for them, and re-layouts: 8.92 us -> 6.74 us
    unnamed x20 -> x12, local copies, waits for them, and re-layouts: 3.04 us -> 0.26 us
where the time goes in v5:
time: 181 us
  starting transfers between devices  63.4 us (35%)
  waiting for transfers between devices  55.9 us (31%)
  blocking collectives  46.2 us (26%)
  local copies, waits for them, and re-layouts  6.74 us (4%)
  matrix products  2.76 us (2%)
  other arithmetic  2.5 us (1%)
  Pallas kernels  2.17 us (1%)
    all_to_all x3, blocking collectives, exchange(): return lax.all_to_all(values, axis, split_axis=0, concat_axis=0, tiled=True)  46.2 us
    all_to_all x2, starting transfers between devices, exchange(): return lax.all_to_all(values, axis, split_axis=0, concat_axis=0, tiled=True)  44.4 us
    all_to_all x2, waiting for transfers between devices, exchange(): return lax.all_to_all(values, axis, split_axis=0, concat_axis=0, tiled=True)  38.4 us
    ppermute x6, starting transfers between devices, swap(): moved.append(lax.ppermute(block_for((me + shift) % size), axis, pairs))  19 us
    ppermute x6, waiting for transfers between devices, swap(): moved.append(lax.ppermute(block_for((me + shift) % size), axis, pairs))  17.5 us
  transfers between devices with their start and end apart: 8, of which 7 were waited for; matrix products, arithmetic and copies ran while one was open for 4% of the time, Pallas kernels for 0%

profile of v5, /device:TPU:1, one launch (start us, length us, event | category | flops | bytes accessed | tf_op | source)
XLA Modules:
  0.0 180.8 jit_solution(18367433638965152241)
XLA Ops:
  0.6 0.0 copy-start.1
  0.7 2.2 %to_slots.1 = bf16[512,256]{1,0:T(8,128)(2,1)} custom-call(s32[8,24]{1,0:T(8,128)} %bitcast.115, f32[8,24]{1,0:T(8,128)} %bitcast.116, bf16[24,256]{1,0:T(8,128)(2,1)} %tokens_ref.1, bf16[24,256]{1,0:T(8,128)(2,1)} %cotangent_ref.1), custom_call_target="tpu_custom_call" | custom-call | flops 25165824 | bytes 262144 | tf_op jit(solution)/shard_map/to_slots/pallas_call | solution.py:86
  2.8 30.4 %all-to-all-start = ((bf16[64,8,256]{2,1,0:T(8,128)(2,1)}), bf16[64,8,256]{2,1,0:T(8,128)(2,1)S(1)}, u32[]{:S(2)}, u32[]{:S(2)}) async-start(bf16[64,8,256]{2,1,0:T(8,128)(2,1)} %bitcast.113), calls=%async_computation | async-start | bytes 524288 | tf_op jit(solution)/shard_map/all_to_all | solution.py:14
  33.3 0.3 concatenate.35
  33.6 0.3 concatenate.36
  33.9 0.3 concatenate.37
  34.2 0.1 copy_dynamic-update-slice_fusion.2
  34.3 0.1 copy_dynamic-update-slice_fusion.1
  34.4 0.0 copy-start.3
  34.4 0.0 copy-start.4
  34.5 0.1 copy_dynamic-update-slice_fusion
  34.6 0.1 dynamic-slice_bitcast_fusion
  34.7 3.1 %collective-permute-start.2 = (bf16[144,4,256]{2,0,1:T(8,128)(2,1)S(1)}, bf16[144,4,256]{2,0,1:T(8,128)(2,1)S(1)}, u32[]{:S(2)}, u32[]{:S(2)}) collective-permute-start(bf16[144,4,256]{2,0,1:T(8,128)(2,1)S(1)} %get-tuple-element.54), channel_id=1, source_target_pairs={{0,1},{1,2},{2,3},{3,0},{4,5},{5,6},{6,7},{7,4},{8,9},{9,10},{10,1... | collective-permute-start | bytes 884744 | tf_op jit(solution)/shard_map/ppermute | solution.py:31
  37.8 4.4 %collective-permute-start.1 = (bf16[144,4,256]{2,0,1:T(8,128)(2,1)S(1)}, bf16[144,4,256]{2,0,1:T(8,128)(2,1)S(1)}, u32[]{:S(2)}, u32[]{:S(2)}) collective-permute-start(bf16[144,4,256]{2,0,1:T(8,128)(2,1)S(1)} %get-tuple-element.55), channel_id=1, source_target_pairs={{0,2},{1,3},{2,0},{3,1},{4,6},{5,7},{6,4},{7,5},{8,10},{9,11},{10,... | collective-permute-start | bytes 884744 | tf_op jit(solution)/shard_map/ppermute | solution.py:31
  42.2 3.1 %collective-permute-start = (bf16[144,4,256]{2,0,1:T(8,128)(2,1)S(1)}, bf16[144,4,256]{2,0,1:T(8,128)(2,1)S(1)}, u32[]{:S(2)}, u32[]{:S(2)}) collective-permute-start(bf16[144,4,256]{2,0,1:T(8,128)(2,1)S(1)} %get-tuple-element.56), channel_id=1, source_target_pairs={{0,3},{1,0},{2,1},{3,2},{4,7},{5,4},{6,5},{7,6},{8,11},{9,8},{10,9... | collective-permute-start | bytes 884744 | tf_op jit(solution)/shard_map/ppermute | solution.py:31
  45.3 0.0 copy-done.3
  45.3 0.1 copy.52
  45.4 0.1 copy.53
  45.5 0.3 fusion.13
  45.8 0.1 compare_select_fusion.1
  45.9 0.0 collective-permute-done.2
  45.9 7.2 %collective-permute-done.1 = bf16[144,4,256]{2,0,1:T(8,128)(2,1)S(1)} collective-permute-done((bf16[144,4,256]{2,0,1:T(8,128)(2,1)S(1)}, bf16[144,4,256]{2,0,1:T(8,128)(2,1)S(1)}, u32[]{:S(2)}, u32[]{:S(2)}) %collective-permute-start.1) | collective-permute-done | bytes 294944 | tf_op jit(solution)/shard_map/ppermute | solution.py:31
  53.2 1.3 collective-permute-done
  54.5 0.1 fusion.27
  54.6 0.2 pad_maximum_fusion
  54.8 19.7 %all-to-all-done = bf16[64,8,256]{2,1,0:T(8,128)(2,1)S(1)} async-done(((bf16[64,8,256]{2,1,0:T(8,128)(2,1)}), bf16[64,8,256]{2,1,0:T(8,128)(2,1)S(1)}, u32[]{:S(2)}, u32[]{:S(2)}) %all-to-all-start) | async-done | bytes 262176 | tf_op jit(solution)/shard_map/all_to_all | solution.py:14
  74.5 0.1 fusion.55
  74.7 0.1 broadcast_in_dim.18
  74.8 16.6 %all_to_all.25 = bf16[4,2,256,256]{3,2,1,0:T(8,128)(2,1)S(1)} all-to-all(bf16[4,2,256,256]{3,2,1,0:T(8,128)(2,1)S(1)} %broadcast_in_dim.18), channel_id=1, replica_groups=mesh['expert'=64,'row'=4,'col'=4] {'row'}, dimensions={0} | all-to-all | bytes 2097152 | tf_op jit(solution)/shard_map/all_to_all | solution.py:14
  91.4 0.3 fusion.4
  91.8 0.4 fusion.3
  92.2 0.1 broadcast_in_dim.19
  92.3 16.6 %all_to_all.26 = bf16[4,4,144,256]{3,2,1,0:T(8,128)(2,1)S(1)} all-to-all(bf16[4,4,144,256]{3,2,1,0:T(8,128)(2,1)S(1)} %broadcast_in_dim.19), channel_id=1, replica_groups=mesh['expert'=64,'row'=4,'col'=4] {'col'}, dimensions={0} | all-to-all | bytes 2359296 | tf_op jit(solution)/shard_map/all_to_all | solution.py:14
  108.9 0.2 convert_reduce_fusion
  109.1 0.1 multiply_convert_fusion.2
  109.2 1.0 fusion
  110.3 12.9 %all_to_all.27 = bf16[4,512,256]{1,2,0:T(8,128)(2,1)S(1)} all-to-all(bf16[4,512,256]{1,2,0:T(8,128)(2,1)S(1)} %fusion), channel_id=1, replica_groups=mesh['expert'=64,'row'=4,'col'=4] {'row'}, dimensions={0} | all-to-all | bytes 2097152 | tf_op jit(solution)/shard_map/all_to_all | solution.py:14
  123.2 0.2 reduce_sum.42
  123.5 0.1 copy.56
  123.6 0.1 copy.57
  123.8 0.8 pad_maximum_fusion.4
  124.6 14.0 %all-to-all-start.4 = ((bf16[64,8,256]{2,1,0:T(8,128)(2,1)}), bf16[64,8,256]{2,1,0:T(8,128)(2,1)S(1)}, u32[]{:S(2)}, u32[]{:S(2)}) async-start(bf16[64,8,256]{2,1,0:T(8,128)(2,1)} %pad_maximum_fusion.4), calls=%async_computation.4 | async-start | bytes 524288 | tf_op jit(solution)/shard_map/all_to_all | solution.py:14
  138.6 0.3 convolution_convert_fusion.1
  138.9 0.4 convolution_convert_fusion
  139.2 0.1 fusion.23
  139.3 2.2 %collective-permute-start.5 = (bf16[144,4,256]{2,0,1:T(8,128)(2,1)S(1)}, bf16[144,4,256]{2,0,1:T(8,128)(2,1)S(1)}, u32[]{:S(2)}, u32[]{:S(2)}) collective-permute-start(bf16[144,4,256]{2,0,1:T(8,128)(2,1)S(1)} %get-tuple-element.51), channel_id=1, source_target_pairs={{0,1},{1,2},{2,3},{3,0},{4,5},{5,6},{6,7},{7,4},{8,9},{9,10},{10,1... | collective-permute-start | bytes 884744 | tf_op jit(solution)/shard_map/ppermute | solution.py:31
  141.5 4.3 %collective-permute-start.3 = (bf16[144,4,256]{2,0,1:T(8,128)(2,1)S(1)}, bf16[144,4,256]{2,0,1:T(8,128)(2,1)S(1)}, u32[]{:S(2)}, u32[]{:S(2)}) collective-permute-start(bf16[144,4,256]{2,0,1:T(8,128)(2,1)S(1)} %get-tuple-element.52), channel_id=1, source_target_pairs={{0,3},{1,0},{2,1},{3,2},{4,7},{5,4},{6,5},{7,6},{8,11},{9,8},{10,9... | collective-permute-start | bytes 884744 | tf_op jit(solution)/shard_map/ppermute | solution.py:31
  145.8 1.9 %collective-permute-start.4 = (bf16[144,4,256]{2,0,1:T(8,128)(2,1)S(1)}, bf16[144,4,256]{2,0,1:T(8,128)(2,1)S(1)}, u32[]{:S(2)}, u32[]{:S(2)}) collective-permute-start(bf16[144,4,256]{2,0,1:T(8,128)(2,1)S(1)} %get-tuple-element.53), channel_id=1, source_target_pairs={{0,2},{1,3},{2,0},{3,1},{4,6},{5,7},{6,4},{7,5},{8,10},{9,11},{10,... | collective-permute-start | bytes 884744 | tf_op jit(solution)/shard_map/ppermute | solution.py:31
  147.8 2.8 %collective-permute-done.5 = bf16[144,4,256]{2,0,1:T(8,128)(2,1)S(1)} collective-permute-done((bf16[144,4,256]{2,0,1:T(8,128)(2,1)S(1)}, bf16[144,4,256]{2,0,1:T(8,128)(2,1)S(1)}, u32[]{:S(2)}, u32[]{:S(2)}) %collective-permute-start.5) | collective-permute-done | bytes 294944 | tf_op jit(solution)/shard_map/ppermute | solution.py:31
  150.6 1.6 collective-permute-done.3
  152.1 4.6 %collective-permute-done.4 = bf16[144,4,256]{2,0,1:T(8,128)(2,1)S(1)} collective-permute-done((bf16[144,4,256]{2,0,1:T(8,128)(2,1)S(1)}, bf16[144,4,256]{2,0,1:T(8,128)(2,1)S(1)}, u32[]{:S(2)}, u32[]{:S(2)}) %collective-permute-start.4) | collective-permute-done | bytes 294944 | tf_op jit(solution)/shard_map/ppermute | solution.py:31
  156.7 0.2 select_bitcast_fusion.3
  156.9 0.1 select_bitcast_fusion.2
  157.0 0.2 pad_maximum_fusion.1
  157.2 0.1 fusion.53
  157.3 0.3 copy.60
  157.6 1.0 squeeze.56
  158.6 0.3 copy.59
  158.9 1.0 squeeze.55
  159.9 0.3 copy.58
  160.2 1.0 squeeze.54
  161.3 18.6 %all-to-all-done.4 = bf16[64,8,256]{2,1,0:T(8,128)(2,1)S(1)} async-done(((bf16[64,8,256]{2,1,0:T(8,128)(2,1)}), bf16[64,8,256]{2,1,0:T(8,128)(2,1)S(1)}, u32[]{:S(2)}, u32[]{:S(2)}) %all-to-all-start.4) | async-done | bytes 262176 | tf_op jit(solution)/shard_map/all_to_all | solution.py:14
  179.9 0.3 convolution_convert_fusion.3
  180.1 0.6 fusion.56
  (16 shorter events, 0.3 us)
Async XLA Ops:
  0.6 32.9 %copy-start.1 = (bf16[1,48,4096]{2,1,0:T(8,128)(2,1)S(1)}, bf16[1,48,4096]{2,1,0:T(8,128)(2,1)}, u32[]{:S(2)}) copy-start(bf16[1,48,4096]{2,1,0:T(8,128)(2,1)} %param.12) | copy-start | bytes 1179652
  0.6 32.6 %copy-start = (bf16[1,48,4096]{2,1,0:T(8,128)(2,1)S(1)}, bf16[1,48,4096]{2,1,0:T(8,128)(2,1)}, u32[]{:S(2)}) copy-start(bf16[1,48,4096]{2,1,0:T(8,128)(2,1)} %param.11) | copy-start | bytes 1179652
  0.7 33.2 %copy-start.2 = (bf16[1,48,4096]{2,1,0:T(8,128)(2,1)S(1)}, bf16[1,48,4096]{2,1,0:T(8,128)(2,1)}, u32[]{:S(2)}) copy-start(bf16[1,48,4096]{2,1,0:T(8,128)(2,1)} %param.13) | copy-start | bytes 1179652
  2.8 71.7 %all-to-all-start = ((bf16[64,8,256]{2,1,0:T(8,128)(2,1)}), bf16[64,8,256]{2,1,0:T(8,128)(2,1)S(1)}, u32[]{:S(2)}, u32[]{:S(2)}) async-start(bf16[64,8,256]{2,1,0:T(8,128)(2,1)} %bitcast.113), calls=%async_computation | async-start | bytes 524288 | tf_op jit(solution)/shard_map/all_to_all | solution.py:14
  34.4 10.9 %copy-start.3 = (s32[24,8]{0,1:T(8,128)S(1)}, s32[24,8]{0,1:T(8,128)}, u32[]{:S(2)}) copy-start(s32[24,8]{0,1:T(8,128)} %param.8) | copy-start | bytes 2308
  34.4 11.0 %copy-start.4 = (f32[24,8]{0,1:T(8,128)S(1)}, f32[24,8]{0,1:T(8,128)}, u32[]{:S(2)}) copy-start(f32[24,8]{0,1:T(8,128)} %param.9) | copy-start | bytes 2308
  34.7 11.3 %collective-permute-start.2 = (bf16[144,4,256]{2,0,1:T(8,128)(2,1)S(1)}, bf16[144,4,256]{2,0,1:T(8,128)(2,1)S(1)}, u32[]{:S(2)}, u32[]{:S(2)}) collective-permute-start(bf16[144,4,256]{2,0,1:T(8,128)(2,1)S(1)} %get-tuple-element.54), channel_id=1, source_target_pairs={{0,1},{1,2},{2,3},{3,0},{4,5},{5,6},{6,7},{7,4},{8,9},{9,10},{10,1... | collective-permute-start | bytes 884744 | tf_op jit(solution)/shard_map/ppermute | solution.py:31
  37.8 15.4 %collective-permute-start.1 = (bf16[144,4,256]{2,0,1:T(8,128)(2,1)S(1)}, bf16[144,4,256]{2,0,1:T(8,128)(2,1)S(1)}, u32[]{:S(2)}, u32[]{:S(2)}) collective-permute-start(bf16[144,4,256]{2,0,1:T(8,128)(2,1)S(1)} %get-tuple-element.55), channel_id=1, source_target_pairs={{0,2},{1,3},{2,0},{3,1},{4,6},{5,7},{6,4},{7,5},{8,10},{9,11},{10,... | collective-permute-start | bytes 884744 | tf_op jit(solution)/shard_map/ppermute | solution.py:31
  42.2 12.3 %collective-permute-start = (bf16[144,4,256]{2,0,1:T(8,128)(2,1)S(1)}, bf16[144,4,256]{2,0,1:T(8,128)(2,1)S(1)}, u32[]{:S(2)}, u32[]{:S(2)}) collective-permute-start(bf16[144,4,256]{2,0,1:T(8,128)(2,1)S(1)} %get-tuple-element.56), channel_id=1, source_target_pairs={{0,3},{1,0},{2,1},{3,2},{4,7},{5,4},{6,5},{7,6},{8,11},{9,8},{10,9... | collective-permute-start | bytes 884744 | tf_op jit(solution)/shard_map/ppermute | solution.py:31
  124.6 55.3 %all-to-all-start.4 = ((bf16[64,8,256]{2,1,0:T(8,128)(2,1)}), bf16[64,8,256]{2,1,0:T(8,128)(2,1)S(1)}, u32[]{:S(2)}, u32[]{:S(2)}) async-start(bf16[64,8,256]{2,1,0:T(8,128)(2,1)} %pad_maximum_fusion.4), calls=%async_computation.4 | async-start | bytes 524288 | tf_op jit(solution)/shard_map/all_to_all | solution.py:14
  139.3 11.2 %collective-permute-start.5 = (bf16[144,4,256]{2,0,1:T(8,128)(2,1)S(1)}, bf16[144,4,256]{2,0,1:T(8,128)(2,1)S(1)}, u32[]{:S(2)}, u32[]{:S(2)}) collective-permute-start(bf16[144,4,256]{2,0,1:T(8,128)(2,1)S(1)} %get-tuple-element.51), channel_id=1, source_target_pairs={{0,1},{1,2},{2,3},{3,0},{4,5},{5,6},{6,7},{7,4},{8,9},{9,10},{10,1... | collective-permute-start | bytes 884744 | tf_op jit(solution)/shard_map/ppermute | solution.py:31
  141.5 10.6 %collective-permute-start.3 = (bf16[144,4,256]{2,0,1:T(8,128)(2,1)S(1)}, bf16[144,4,256]{2,0,1:T(8,128)(2,1)S(1)}, u32[]{:S(2)}, u32[]{:S(2)}) collective-permute-start(bf16[144,4,256]{2,0,1:T(8,128)(2,1)S(1)} %get-tuple-element.52), channel_id=1, source_target_pairs={{0,3},{1,0},{2,1},{3,2},{4,7},{5,4},{6,5},{7,6},{8,11},{9,8},{10,9... | collective-permute-start | bytes 884744 | tf_op jit(solution)/shard_map/ppermute | solution.py:31
  145.8 10.9 %collective-permute-start.4 = (bf16[144,4,256]{2,0,1:T(8,128)(2,1)S(1)}, bf16[144,4,256]{2,0,1:T(8,128)(2,1)S(1)}, u32[]{:S(2)}, u32[]{:S(2)}) collective-permute-start(bf16[144,4,256]{2,0,1:T(8,128)(2,1)S(1)} %get-tuple-element.53), channel_id=1, source_target_pairs={{0,2},{1,3},{2,0},{3,1},{4,6},{5,7},{6,4},{7,5},{8,10},{9,11},{10,... | collective-permute-start | bytes 884744 | tf_op jit(solution)/shard_map/ppermute | solution.py:31

commit v6 on v5

--- a/solution.py
+++ b/solution.py
@@ -55,12 +55,12 @@
 def to_slots_kernel(routes_ref, gates_ref, tokens_ref, cotangent_ref, sent_ref):
     tops, count = routes_ref.shape
     slots = sent_ref.shape[0]
+    experts = slots // (2 * CAP)
     listed, weights = (jnp.concatenate([ref[...]] * 4, axis=1) for ref in (routes_ref, gates_ref))
-    slot = lax.broadcasted_iota(jnp.int32, (slots, 4 * count), 0)
-    column = lax.broadcasted_iota(jnp.int32, (slots, 4 * count), 1)
-    expert, place = slot // (2 * CAP), slot % (2 * CAP)
-    named = jnp.zeros((slots, 4 * count), F32)
-    weight = jnp.zeros((slots, 4 * count), F32)
+    expert = lax.broadcasted_iota(jnp.int32, (experts, 4 * count), 0)
+    section = lax.broadcasted_iota(jnp.int32, (experts, 4 * count), 1) // count
+    named = jnp.zeros((experts, 4 * count), F32)
+    weight = jnp.zeros((experts, 4 * count), F32)
     for k in range(tops):
         chosen = listed[k : k + 1] == expert
         named = jnp.where(chosen, 1.0, named)
@@ -69,13 +69,17 @@
     later = lax.broadcasted_iota(jnp.int32, (4 * count, 4 * count), 1)
     before = ((earlier < later) & (earlier // count == later // count)).astype(F32).astype(BF16)
     position = jnp.dot(named.astype(BF16), before, preferred_element_type=F32).astype(jnp.int32)
-    section = column // count
     high = weight.astype(BF16).astype(F32)
     middle = (weight - high).astype(BF16).astype(F32)
     low = weight - high - middle
-    part = jnp.where(section == 0, 1.0, jnp.where(section == 1, high, jnp.where(section == 2, middle, low)))
+    part = jnp.where(section == 0, named, jnp.where(section == 1, high, jnp.where(section == 2, middle, low)))
     wanted = position + jnp.where(section == 0, 0, CAP)
-    spread = jnp.where((named > 0.0) & (wanted == place), part, 0.0).astype(BF16)
+
+    def over_slots(values):
+        return jnp.broadcast_to(values[:, None], (experts, 2 * CAP, 4 * count)).reshape(slots, 4 * count)
+
+    place = lax.broadcasted_iota(jnp.int32, (slots, 4 * count), 0) % (2 * CAP)
+    spread = jnp.where(over_slots(wanted) == place, over_slots(part), 0.0).astype(BF16)
     cotangents = cotangent_ref[...].astype(F32)
     sources = jnp.concatenate([tokens_ref[...].astype(F32)] + [cotangents] * 3).astype(BF16)
     sent_ref[...] = jnp.dot(spread, sources, preferred_element_type=F32).astype(BF16)
@@ -140,7 +144,7 @@
         ],
         axis=2,
     )
-    results = product(blocks, weights, "shr,shyf->yrf").astype(BF16)
+    results = product(blocks, weights, "shr,shyf->ryf").astype(BF16).swapaxes(0, 1)
     results = jnp.sum(exchange(results, "row").astype(F32), axis=0).astype(BF16)
     returned = jnp.concatenate(
         [results[:rows].reshape(experts, CAP, width), results[rows:].reshape(experts, CAP, width)], axis=1

time: 181 us -> 181 us (level)
  no operation moved by 1% of the time
where the time goes in v6:
time: 181 us; the launch traced here: 180 us
  starting transfers between devices  63.4 us (35%)
  waiting for transfers between devices  55.9 us (31%)
  blocking collectives  46.2 us (26%)
  local copies, waits for them, and re-layouts  6.54 us (4%)
  matrix products  2.76 us (2%)
  other arithmetic  2.52 us (1%)
  Pallas kernels  1.99 us (1%)
    all_to_all x3, blocking collectives, exchange(): return lax.all_to_all(values, axis, split_axis=0, concat_axis=0, tiled=True)  46.2 us
    all_to_all x2, starting transfers between devices, exchange(): return lax.all_to_all(values, axis, split_axis=0, concat_axis=0, tiled=True)  44.4 us
    all_to_all x2, waiting for transfers between devices, exchange(): return lax.all_to_all(values, axis, split_axis=0, concat_axis=0, tiled=True)  38.4 us
    ppermute x6, starting transfers between devices, swap(): moved.append(lax.ppermute(block_for((me + shift) % size), axis, pairs))  19 us
    ppermute x6, waiting for transfers between devices, swap(): moved.append(lax.ppermute(block_for((me + shift) % size), axis, pairs))  17.5 us
  transfers between devices with their start and end apart: 8, of which 7 were waited for; matrix products, arithmetic and copies ran while one was open for 4% of the time, Pallas kernels for 0%

profile of v6, /device:TPU:1, one launch (start us, length us, event | category | flops | bytes accessed | tf_op | source)
XLA Modules:
  0.0 180.4 jit_solution(8115997577423419665)
XLA Ops:
  0.6 0.0 copy-start.1
  0.6 0.0 copy-start
  0.7 0.0 copy-start.2
  0.7 2.0 %to_slots.1 = bf16[512,256]{1,0:T(8,128)(2,1)} custom-call(s32[8,24]{1,0:T(8,128)} %bitcast.118, f32[8,24]{1,0:T(8,128)} %bitcast.119, bf16[24,256]{1,0:T(8,128)(2,1)} %tokens_ref.1, bf16[24,256]{1,0:T(8,128)(2,1)} %cotangent_ref.1), custom_call_target="tpu_custom_call" | custom-call | flops 25165824 | bytes 262144 | tf_op jit(solution)/shard_map/to_slots/pallas_call | solution.py:90
  2.7 30.4 %all-to-all-start = ((bf16[64,8,256]{2,1,0:T(8,128)(2,1)}), bf16[64,8,256]{2,1,0:T(8,128)(2,1)S(1)}, u32[]{:S(2)}, u32[]{:S(2)}) async-start(bf16[64,8,256]{2,1,0:T(8,128)(2,1)} %bitcast.116), calls=%async_computation | async-start | bytes 524288 | tf_op jit(solution)/shard_map/all_to_all | solution.py:14
  33.1 0.3 concatenate.35
  33.4 0.0 copy-done.1
  33.4 0.3 concatenate.36
  33.7 0.3 concatenate.37
  34.0 0.1 copy_dynamic-update-slice_fusion.2
  34.1 0.1 copy_dynamic-update-slice_fusion.1
  34.3 0.0 copy-start.3
  34.3 0.0 copy-start.4
  34.3 0.1 copy_dynamic-update-slice_fusion
  34.4 0.1 dynamic-slice_bitcast_fusion
  34.5 3.1 %collective-permute-start.2 = (bf16[144,4,256]{2,0,1:T(8,128)(2,1)S(1)}, bf16[144,4,256]{2,0,1:T(8,128)(2,1)S(1)}, u32[]{:S(2)}, u32[]{:S(2)}) collective-permute-start(bf16[144,4,256]{2,0,1:T(8,128)(2,1)S(1)} %get-tuple-element.54), channel_id=1, source_target_pairs={{0,1},{1,2},{2,3},{3,0},{4,5},{5,6},{6,7},{7,4},{8,9},{9,10},{10,1... | collective-permute-start | bytes 884744 | tf_op jit(solution)/shard_map/ppermute | solution.py:31
  37.6 4.4 %collective-permute-start.1 = (bf16[144,4,256]{2,0,1:T(8,128)(2,1)S(1)}, bf16[144,4,256]{2,0,1:T(8,128)(2,1)S(1)}, u32[]{:S(2)}, u32[]{:S(2)}) collective-permute-start(bf16[144,4,256]{2,0,1:T(8,128)(2,1)S(1)} %get-tuple-element.55), channel_id=1, source_target_pairs={{0,2},{1,3},{2,0},{3,1},{4,6},{5,7},{6,4},{7,5},{8,10},{9,11},{10,... | collective-permute-start | bytes 884744 | tf_op jit(solution)/shard_map/ppermute | solution.py:31
  42.0 3.1 %collective-permute-start = (bf16[144,4,256]{2,0,1:T(8,128)(2,1)S(1)}, bf16[144,4,256]{2,0,1:T(8,128)(2,1)S(1)}, u32[]{:S(2)}, u32[]{:S(2)}) collective-permute-start(bf16[144,4,256]{2,0,1:T(8,128)(2,1)S(1)} %get-tuple-element.56), channel_id=1, source_target_pairs={{0,3},{1,0},{2,1},{3,2},{4,7},{5,4},{6,5},{7,6},{8,11},{9,8},{10,9... | collective-permute-start | bytes 884744 | tf_op jit(solution)/shard_map/ppermute | solution.py:31
  45.1 0.1 copy.41
  45.2 0.1 copy.42
  45.3 0.3 fusion.13
  45.6 0.1 compare_select_fusion.1
  45.8 0.0 collective-permute-done.2
  45.8 7.3 %collective-permute-done.1 = bf16[144,4,256]{2,0,1:T(8,128)(2,1)S(1)} collective-permute-done((bf16[144,4,256]{2,0,1:T(8,128)(2,1)S(1)}, bf16[144,4,256]{2,0,1:T(8,128)(2,1)S(1)}, u32[]{:S(2)}, u32[]{:S(2)}) %collective-permute-start.1) | collective-permute-done | bytes 294944 | tf_op jit(solution)/shard_map/ppermute | solution.py:31
  53.0 1.3 collective-permute-done
  54.3 0.1 fusion.27
  54.5 0.2 pad_maximum_fusion
  54.6 19.7 %all-to-all-done = bf16[64,8,256]{2,1,0:T(8,128)(2,1)S(1)} async-done(((bf16[64,8,256]{2,1,0:T(8,128)(2,1)}), bf16[64,8,256]{2,1,0:T(8,128)(2,1)S(1)}, u32[]{:S(2)}, u32[]{:S(2)}) %all-to-all-start) | async-done | bytes 262176 | tf_op jit(solution)/shard_map/all_to_all | solution.py:14
  74.4 0.1 fusion.55
  74.6 0.1 broadcast_in_dim.18
  74.6 16.6 %all_to_all.25 = bf16[4,2,256,256]{3,2,1,0:T(8,128)(2,1)S(1)} all-to-all(bf16[4,2,256,256]{3,2,1,0:T(8,128)(2,1)S(1)} %broadcast_in_dim.18), channel_id=1, replica_groups=mesh['expert'=64,'row'=4,'col'=4] {'row'}, dimensions={0} | all-to-all | bytes 2097152 | tf_op jit(solution)/shard_map/all_to_all | solution.py:14
  91.2 0.3 fusion.4
  91.6 0.4 fusion.3
  92.0 0.1 broadcast_in_dim.19
  92.1 16.6 %all_to_all.26 = bf16[4,4,144,256]{3,2,1,0:T(8,128)(2,1)S(1)} all-to-all(bf16[4,4,144,256]{3,2,1,0:T(8,128)(2,1)S(1)} %broadcast_in_dim.19), channel_id=1, replica_groups=mesh['expert'=64,'row'=4,'col'=4] {'col'}, dimensions={0} | all-to-all | bytes 2359296 | tf_op jit(solution)/shard_map/all_to_all | solution.py:14
  108.7 0.2 convert_reduce_fusion
  108.9 0.1 multiply_convert_fusion.2
  109.1 1.0 fusion
  110.1 12.9 %all_to_all.27 = bf16[4,512,256]{2,1,0:T(8,128)(2,1)S(1)} all-to-all(bf16[4,512,256]{2,1,0:T(8,128)(2,1)S(1)} %fusion), channel_id=1, replica_groups=mesh['expert'=64,'row'=4,'col'=4] {'row'}, dimensions={0} | all-to-all | bytes 2097152 | tf_op jit(solution)/shard_map/all_to_all | solution.py:14
  123.0 0.3 reduce_sum.42
  123.4 0.8 pad_maximum_fusion.4
  124.2 14.0 %all-to-all-start.4 = ((bf16[64,8,256]{2,1,0:T(8,128)(2,1)}), bf16[64,8,256]{2,1,0:T(8,128)(2,1)S(1)}, u32[]{:S(2)}, u32[]{:S(2)}) async-start(bf16[64,8,256]{2,1,0:T(8,128)(2,1)} %pad_maximum_fusion.4), calls=%async_computation.4 | async-start | bytes 524288 | tf_op jit(solution)/shard_map/all_to_all | solution.py:14
  138.2 0.3 convolution_convert_fusion.1
  138.5 0.4 convolution_convert_fusion
  138.9 0.1 fusion.23
  138.9 2.2 %collective-permute-start.5 = (bf16[144,4,256]{2,0,1:T(8,128)(2,1)S(1)}, bf16[144,4,256]{2,0,1:T(8,128)(2,1)S(1)}, u32[]{:S(2)}, u32[]{:S(2)}) collective-permute-start(bf16[144,4,256]{2,0,1:T(8,128)(2,1)S(1)} %get-tuple-element.51), channel_id=1, source_target_pairs={{0,1},{1,2},{2,3},{3,0},{4,5},{5,6},{6,7},{7,4},{8,9},{9,10},{10,1... | collective-permute-start | bytes 884744 | tf_op jit(solution)/shard_map/ppermute | solution.py:31
  141.1 4.3 %collective-permute-start.3 = (bf16[144,4,256]{2,0,1:T(8,128)(2,1)S(1)}, bf16[144,4,256]{2,0,1:T(8,128)(2,1)S(1)}, u32[]{:S(2)}, u32[]{:S(2)}) collective-permute-start(bf16[144,4,256]{2,0,1:T(8,128)(2,1)S(1)} %get-tuple-element.52), channel_id=1, source_target_pairs={{0,3},{1,0},{2,1},{3,2},{4,7},{5,4},{6,5},{7,6},{8,11},{9,8},{10,9... | collective-permute-start | bytes 884744 | tf_op jit(solution)/shard_map/ppermute | solution.py:31
  145.4 1.9 %collective-permute-start.4 = (bf16[144,4,256]{2,0,1:T(8,128)(2,1)S(1)}, bf16[144,4,256]{2,0,1:T(8,128)(2,1)S(1)}, u32[]{:S(2)}, u32[]{:S(2)}) collective-permute-start(bf16[144,4,256]{2,0,1:T(8,128)(2,1)S(1)} %get-tuple-element.53), channel_id=1, source_target_pairs={{0,2},{1,3},{2,0},{3,1},{4,6},{5,7},{6,4},{7,5},{8,10},{9,11},{10,... | collective-permute-start | bytes 884744 | tf_op jit(solution)/shard_map/ppermute | solution.py:31
  147.4 2.8 %collective-permute-done.5 = bf16[144,4,256]{2,0,1:T(8,128)(2,1)S(1)} collective-permute-done((bf16[144,4,256]{2,0,1:T(8,128)(2,1)S(1)}, bf16[144,4,256]{2,0,1:T(8,128)(2,1)S(1)}, u32[]{:S(2)}, u32[]{:S(2)}) %collective-permute-start.5) | collective-permute-done | bytes 294944 | tf_op jit(solution)/shard_map/ppermute | solution.py:31
  150.2 1.6 collective-permute-done.3
  151.7 4.6 %collective-permute-done.4 = bf16[144,4,256]{2,0,1:T(8,128)(2,1)S(1)} collective-permute-done((bf16[144,4,256]{2,0,1:T(8,128)(2,1)S(1)}, bf16[144,4,256]{2,0,1:T(8,128)(2,1)S(1)}, u32[]{:S(2)}, u32[]{:S(2)}) %collective-permute-start.4) | collective-permute-done | bytes 294944 | tf_op jit(solution)/shard_map/ppermute | solution.py:31
  156.3 0.2 select_bitcast_fusion.3
  156.5 0.1 select_bitcast_fusion.2
  156.6 0.2 pad_maximum_fusion.1
  156.8 0.1 fusion.53
  156.9 0.3 copy.48
  157.2 1.0 squeeze.56
  158.2 0.3 copy.47
  158.5 1.0 squeeze.55
  159.5 0.3 copy.46
  159.9 1.0 squeeze.54
  160.9 18.6 %all-to-all-done.4 = bf16[64,8,256]{2,1,0:T(8,128)(2,1)S(1)} async-done(((bf16[64,8,256]{2,1,0:T(8,128)(2,1)}), bf16[64,8,256]{2,1,0:T(8,128)(2,1)S(1)}, u32[]{:S(2)}, u32[]{:S(2)}) %all-to-all-start.4) | async-done | bytes 262176 | tf_op jit(solution)/shard_map/all_to_all | solution.py:14
  179.5 0.3 convolution_convert_fusion.3
  179.8 0.6 fusion.56
  (14 shorter events, 0.3 us)
Async XLA Ops:
  0.6 32.8 %copy-start.1 = (bf16[1,48,4096]{2,1,0:T(8,128)(2,1)S(1)}, bf16[1,48,4096]{2,1,0:T(8,128)(2,1)}, u32[]{:S(2)}) copy-start(bf16[1,48,4096]{2,1,0:T(8,128)(2,1)} %param.12) | copy-start | bytes 1179652
  0.6 32.5 %copy-start = (bf16[1,48,4096]{2,1,0:T(8,128)(2,1)S(1)}, bf16[1,48,4096]{2,1,0:T(8,128)(2,1)}, u32[]{:S(2)}) copy-start(bf16[1,48,4096]{2,1,0:T(8,128)(2,1)} %param.11) | copy-start | bytes 1179652
  0.7 33.0 %copy-start.2 = (bf16[1,48,4096]{2,1,0:T(8,128)(2,1)S(1)}, bf16[1,48,4096]{2,1,0:T(8,128)(2,1)}, u32[]{:S(2)}) copy-start(bf16[1,48,4096]{2,1,0:T(8,128)(2,1)} %param.13) | copy-start | bytes 1179652
  2.7 71.7 %all-to-all-start = ((bf16[64,8,256]{2,1,0:T(8,128)(2,1)}), bf16[64,8,256]{2,1,0:T(8,128)(2,1)S(1)}, u32[]{:S(2)}, u32[]{:S(2)}) async-start(bf16[64,8,256]{2,1,0:T(8,128)(2,1)} %bitcast.116), calls=%async_computation | async-start | bytes 524288 | tf_op jit(solution)/shard_map/all_to_all | solution.py:14
  34.3 10.9 %copy-start.3 = (s32[24,8]{0,1:T(8,128)S(1)}, s32[24,8]{0,1:T(8,128)}, u32[]{:S(2)}) copy-start(s32[24,8]{0,1:T(8,128)} %param.8) | copy-start | bytes 2308
  34.3 10.9 %copy-start.4 = (f32[24,8]{0,1:T(8,128)S(1)}, f32[24,8]{0,1:T(8,128)}, u32[]{:S(2)}) copy-start(f32[24,8]{0,1:T(8,128)} %param.9) | copy-start | bytes 2308
  34.5 11.3 %collective-permute-start.2 = (bf16[144,4,256]{2,0,1:T(8,128)(2,1)S(1)}, bf16[144,4,256]{2,0,1:T(8,128)(2,1)S(1)}, u32[]{:S(2)}, u32[]{:S(2)}) collective-permute-start(bf16[144,4,256]{2,0,1:T(8,128)(2,1)S(1)} %get-tuple-element.54), channel_id=1, source_target_pairs={{0,1},{1,2},{2,3},{3,0},{4,5},{5,6},{6,7},{7,4},{8,9},{9,10},{10,1... | collective-permute-start | bytes 884744 | tf_op jit(solution)/shard_map/ppermute | solution.py:31
  37.6 15.4 %collective-permute-start.1 = (bf16[144,4,256]{2,0,1:T(8,128)(2,1)S(1)}, bf16[144,4,256]{2,0,1:T(8,128)(2,1)S(1)}, u32[]{:S(2)}, u32[]{:S(2)}) collective-permute-start(bf16[144,4,256]{2,0,1:T(8,128)(2,1)S(1)} %get-tuple-element.55), channel_id=1, source_target_pairs={{0,2},{1,3},{2,0},{3,1},{4,6},{5,7},{6,4},{7,5},{8,10},{9,11},{10,... | collective-permute-start | bytes 884744 | tf_op jit(solution)/shard_map/ppermute | solution.py:31
  42.0 12.3 %collective-permute-start = (bf16[144,4,256]{2,0,1:T(8,128)(2,1)S(1)}, bf16[144,4,256]{2,0,1:T(8,128)(2,1)S(1)}, u32[]{:S(2)}, u32[]{:S(2)}) collective-permute-start(bf16[144,4,256]{2,0,1:T(8,128)(2,1)S(1)} %get-tuple-element.56), channel_id=1, source_target_pairs={{0,3},{1,0},{2,1},{3,2},{4,7},{5,4},{6,5},{7,6},{8,11},{9,8},{10,9... | collective-permute-start | bytes 884744 | tf_op jit(solution)/shard_map/ppermute | solution.py:31
  124.2 55.3 %all-to-all-start.4 = ((bf16[64,8,256]{2,1,0:T(8,128)(2,1)}), bf16[64,8,256]{2,1,0:T(8,128)(2,1)S(1)}, u32[]{:S(2)}, u32[]{:S(2)}) async-start(bf16[64,8,256]{2,1,0:T(8,128)(2,1)} %pad_maximum_fusion.4), calls=%async_computation.4 | async-start | bytes 524288 | tf_op jit(solution)/shard_map/all_to_all | solution.py:14
  138.9 11.2 %collective-permute-start.5 = (bf16[144,4,256]{2,0,1:T(8,128)(2,1)S(1)}, bf16[144,4,256]{2,0,1:T(8,128)(2,1)S(1)}, u32[]{:S(2)}, u32[]{:S(2)}) collective-permute-start(bf16[144,4,256]{2,0,1:T(8,128)(2,1)S(1)} %get-tuple-element.51), channel_id=1, source_target_pairs={{0,1},{1,2},{2,3},{3,0},{4,5},{5,6},{6,7},{7,4},{8,9},{9,10},{10,1... | collective-permute-start | bytes 884744 | tf_op jit(solution)/shard_map/ppermute | solution.py:31
  141.1 10.6 %collective-permute-start.3 = (bf16[144,4,256]{2,0,1:T(8,128)(2,1)S(1)}, bf16[144,4,256]{2,0,1:T(8,128)(2,1)S(1)}, u32[]{:S(2)}, u32[]{:S(2)}) collective-permute-start(bf16[144,4,256]{2,0,1:T(8,128)(2,1)S(1)} %get-tuple-element.52), channel_id=1, source_target_pairs={{0,3},{1,0},{2,1},{3,2},{4,7},{5,4},{6,5},{7,6},{8,11},{9,8},{10,9... | collective-permute-start | bytes 884744 | tf_op jit(solution)/shard_map/ppermute | solution.py:31
  145.4 10.9 %collective-permute-start.4 = (bf16[144,4,256]{2,0,1:T(8,128)(2,1)S(1)}, bf16[144,4,256]{2,0,1:T(8,128)(2,1)S(1)}, u32[]{:S(2)}, u32[]{:S(2)}) collective-permute-start(bf16[144,4,256]{2,0,1:T(8,128)(2,1)S(1)} %get-tuple-element.53), channel_id=1, source_target_pairs={{0,2},{1,3},{2,0},{3,1},{4,6},{5,7},{6,4},{7,5},{8,10},{9,11},{10,... | collective-permute-start | bytes 884744 | tf_op jit(solution)/shard_map/ppermute | solution.py:31

commit v7 on v6

--- a/solution.py
+++ b/solution.py
@@ -129,13 +129,14 @@
         ],
         axis=1,
     )
-    summed = jnp.sum(share(partial, "col").astype(F32), axis=0)
-    gate_pre, up_pre, hidden_grad = summed[:, :units], summed[:, units : 2 * units], summed[:, 2 * units :]
+    summed = jnp.sum(exchange(partial, "col").astype(F32), axis=0)
+    gate_pre, up_pre, hidden_grad = summed[:units], summed[units : 2 * units], summed[2 * units :]
     sigmoid = jax.nn.sigmoid(gate_pre)
     active = gate_pre * sigmoid
     slope = sigmoid * (1.0 + gate_pre * (1.0 - sigmoid))
-    deltas = jnp.concatenate([hidden_grad * up_pre * slope, hidden_grad * active], axis=1).astype(BF16)
-    hidden = (active * up_pre).astype(BF16)
+    mine = jnp.concatenate([hidden_grad * up_pre * slope, hidden_grad * active, active * up_pre]).astype(BF16)
+    whole = share(mine, "col")
+    deltas, hidden = whole[:, : 2 * units], whole[:, 2 * units :]
 
     blocks = jnp.concatenate(
         [

time: 181 us -> 182 us (level)
  blocking collectives: 46.2 us -> 34.3 us
  waiting for transfers between devices: 55.9 us -> 65.5 us
  starting transfers between devices: 63.4 us -> 65.6 us
    all_to_all x3, blocking collectives: 46.2 us -> 34.3 us  [exchange(): return lax.all_to_all(values, axis, split_axis=0, concat_axis=0, tiled=True)]
    all_to_all x2 -> x3, waiting for transfers between devices: 38.4 us -> 48 us  [exchange(): return lax.all_to_all(values, axis, split_axis=0, concat_axis=0, tiled=True)]
    all_to_all x2 -> x3, starting transfers between devices: 44.4 us -> 46.7 us  [exchange(): return lax.all_to_all(values, axis, split_axis=0, concat_axis=0, tiled=True)]
  transfers between devices with their start and end apart: 8 -> 9, of which waited for: 7 -> 8; matrix products, arithmetic and copies ran while one was open for 4% -> 4% of each run, Pallas kernels for 0% -> 0%
where the time goes in v7:
time: 182 us; the launch traced here: 181 us
  starting transfers between devices  65.6 us (36%)
  waiting for transfers between devices  65.5 us (36%)
  blocking collectives  34.3 us (19%)
  local copies, waits for them, and re-layouts  6.52 us (4%)
  matrix products  3.74 us (2%)
  other arithmetic  2.41 us (1%)
  Pallas kernels  1.99 us (1%)
    all_to_all x3, waiting for transfers between devices, exchange(): return lax.all_to_all(values, axis, split_axis=0, concat_axis=0, tiled=True)  48 us
    all_to_all x3, starting transfers between devices, exchange(): return lax.all_to_all(values, axis, split_axis=0, concat_axis=0, tiled=True)  46.7 us
    all_to_all x3, blocking collectives, exchange(): return lax.all_to_all(values, axis, split_axis=0, concat_axis=0, tiled=True)  34.3 us
    ppermute x6, starting transfers between devices, swap(): moved.append(lax.ppermute(block_for((me + shift) % size), axis, pairs))  19 us
    ppermute x6, waiting for transfers between devices, swap(): moved.append(lax.ppermute(block_for((me + shift) % size), axis, pairs))  17.5 us
  transfers between devices with their start and end apart: 9, of which 8 were waited for; matrix products, arithmetic and copies ran while one was open for 4% of the time, Pallas kernels for 0%

profile of v7, /device:TPU:1, one launch (start us, length us, event | category | flops | bytes accessed | tf_op | source)
XLA Modules:
  0.0 181.4 jit_solution(2111053304254694446)
XLA Ops:
  0.6 0.0 copy-start.4
  0.6 0.0 copy-start.3
  0.7 2.0 %to_slots.1 = bf16[512,256]{1,0:T(8,128)(2,1)} custom-call(s32[8,24]{1,0:T(8,128)} %bitcast.118, f32[8,24]{1,0:T(8,128)} %bitcast.119, bf16[24,256]{1,0:T(8,128)(2,1)} %tokens_ref.1, bf16[24,256]{1,0:T(8,128)(2,1)} %cotangent_ref.1), custom_call_target="tpu_custom_call" | custom-call | flops 25165824 | bytes 262144 | tf_op jit(solution)/shard_map/to_slots/pallas_call | solution.py:90
  2.7 30.4 %all-to-all-start = ((bf16[64,8,256]{2,1,0:T(8,128)(2,1)}), bf16[64,8,256]{2,1,0:T(8,128)(2,1)S(1)}, u32[]{:S(2)}, u32[]{:S(2)}) async-start(bf16[64,8,256]{2,1,0:T(8,128)(2,1)} %bitcast.116), calls=%async_computation | async-start | bytes 524288 | tf_op jit(solution)/shard_map/all_to_all | solution.py:14
  33.1 0.3 concatenate.39
  33.4 0.3 concatenate.40
  33.7 0.3 concatenate.41
  34.0 0.1 copy_dynamic-update-slice_fusion.2
  34.1 0.1 copy_dynamic-update-slice_fusion.1
  34.3 0.0 copy-start.6
  34.3 0.0 copy-start.7
  34.3 0.1 copy_dynamic-update-slice_fusion
  34.4 0.1 dynamic-slice_bitcast_fusion
  34.5 3.1 %collective-permute-start.2 = (bf16[144,4,256]{2,0,1:T(8,128)(2,1)S(1)}, bf16[144,4,256]{2,0,1:T(8,128)(2,1)S(1)}, u32[]{:S(2)}, u32[]{:S(2)}) collective-permute-start(bf16[144,4,256]{2,0,1:T(8,128)(2,1)S(1)} %get-tuple-element.54), channel_id=1, source_target_pairs={{0,1},{1,2},{2,3},{3,0},{4,5},{5,6},{6,7},{7,4},{8,9},{9,10},{10,1... | collective-permute-start | bytes 884744 | tf_op jit(solution)/shard_map/ppermute | solution.py:31
  37.6 4.4 %collective-permute-start.1 = (bf16[144,4,256]{2,0,1:T(8,128)(2,1)S(1)}, bf16[144,4,256]{2,0,1:T(8,128)(2,1)S(1)}, u32[]{:S(2)}, u32[]{:S(2)}) collective-permute-start(bf16[144,4,256]{2,0,1:T(8,128)(2,1)S(1)} %get-tuple-element.55), channel_id=1, source_target_pairs={{0,2},{1,3},{2,0},{3,1},{4,6},{5,7},{6,4},{7,5},{8,10},{9,11},{10,... | collective-permute-start | bytes 884744 | tf_op jit(solution)/shard_map/ppermute | solution.py:31
  42.0 3.1 %collective-permute-start = (bf16[144,4,256]{2,0,1:T(8,128)(2,1)S(1)}, bf16[144,4,256]{2,0,1:T(8,128)(2,1)S(1)}, u32[]{:S(2)}, u32[]{:S(2)}) collective-permute-start(bf16[144,4,256]{2,0,1:T(8,128)(2,1)S(1)} %get-tuple-element.56), channel_id=1, source_target_pairs={{0,3},{1,0},{2,1},{3,2},{4,7},{5,4},{6,5},{7,6},{8,11},{9,8},{10,9... | collective-permute-start | bytes 884744 | tf_op jit(solution)/shard_map/ppermute | solution.py:31
  45.1 0.1 copy.41
  45.2 0.1 copy.42
  45.3 0.3 fusion.11
  45.6 0.1 compare_select_fusion.1
  45.8 0.0 collective-permute-done.2
  45.8 7.3 %collective-permute-done.1 = bf16[144,4,256]{2,0,1:T(8,128)(2,1)S(1)} collective-permute-done((bf16[144,4,256]{2,0,1:T(8,128)(2,1)S(1)}, bf16[144,4,256]{2,0,1:T(8,128)(2,1)S(1)}, u32[]{:S(2)}, u32[]{:S(2)}) %collective-permute-start.1) | collective-permute-done | bytes 294944 | tf_op jit(solution)/shard_map/ppermute | solution.py:31
  53.0 1.3 collective-permute-done
  54.3 0.1 fusion.25
  54.5 0.2 pad_maximum_fusion
  54.6 19.7 %all-to-all-done = bf16[64,8,256]{2,1,0:T(8,128)(2,1)S(1)} async-done(((bf16[64,8,256]{2,1,0:T(8,128)(2,1)}), bf16[64,8,256]{2,1,0:T(8,128)(2,1)S(1)}, u32[]{:S(2)}, u32[]{:S(2)}) %all-to-all-start) | async-done | bytes 262176 | tf_op jit(solution)/shard_map/all_to_all | solution.py:14
  74.4 0.1 fusion.53
  74.6 0.1 broadcast_in_dim.18
  74.6 16.6 %all_to_all.30 = bf16[4,2,256,256]{3,2,1,0:T(8,128)(2,1)S(1)} all-to-all(bf16[4,2,256,256]{3,2,1,0:T(8,128)(2,1)S(1)} %broadcast_in_dim.18), channel_id=1, replica_groups=mesh['expert'=64,'row'=4,'col'=4] {'row'}, dimensions={0} | all-to-all | bytes 2097152 | tf_op jit(solution)/shard_map/all_to_all | solution.py:14
  91.2 0.3 fusion.3
  91.6 0.4 fusion.2
  92.0 0.0 copy-start.8
  92.0 9.5 %all_to_all.31 = bf16[4,144,256]{2,1,0:T(8,128)(2,1)S(1)} all-to-all(bf16[4,144,256]{2,1,0:T(8,128)(2,1)S(1)} %pad_maximum_fusion.2), channel_id=1, replica_groups=mesh['expert'=64,'row'=4,'col'=4] {'col'}, dimensions={0} | all-to-all | bytes 589824 | tf_op jit(solution)/shard_map/all_to_all | solution.py:14
  101.7 8.2 %all_to_all.32 = bf16[4,144,256]{2,1,0:T(8,128)(2,1)S(1)} all-to-all(bf16[4,144,256]{2,1,0:T(8,128)(2,1)S(1)} %broadcast_in_dim.19), channel_id=1, replica_groups=mesh['expert'=64,'row'=4,'col'=4] {'col'}, dimensions={0} | all-to-all | bytes 589824 | tf_op jit(solution)/shard_map/all_to_all | solution.py:14
  109.9 0.1 broadcast_select_fusion
  110.0 2.0 %fusion = bf16[4,512,256]{2,1,0:T(8,128)(2,1)} fusion(bf16[4,144,4,256]{3,1,2,0:T(8,128)(2,1)S(1)} %copy-done.2, bf16[4,48,256]{2,1,0:T(8,128)(2,1)S(1)} %slice.81, bf16[4,144,256]{2,1,0:T(8,128)(2,1)S(1)} %broadcast_select_fusion), kind=kOutput, calls=%fused_computation.6 | convolution fusion | flops 606273536 | bytes 2621440 | tf_op jit(solution)/shard_map/shr,shyf->ryf/dot_general | solution.py:23
  112.0 3.5 %all-to-all-start.4 = ((bf16[4,512,256]{2,1,0:T(8,128)(2,1)}), bf16[4,512,256]{2,1,0:T(8,128)(2,1)S(1)}, u32[]{:S(2)}, u32[]{:S(2)}) async-start(bf16[4,512,256]{2,1,0:T(8,128)(2,1)} %fusion), calls=%async_computation.4 | async-start | bytes 2097152 | tf_op jit(solution)/shard_map/all_to_all | solution.py:14
  115.5 9.7 %all-to-all-done.4 = bf16[4,512,256]{2,1,0:T(8,128)(2,1)S(1)} async-done(((bf16[4,512,256]{2,1,0:T(8,128)(2,1)}), bf16[4,512,256]{2,1,0:T(8,128)(2,1)S(1)}, u32[]{:S(2)}, u32[]{:S(2)}) %all-to-all-start.4) | async-done | bytes 1048608 | tf_op jit(solution)/shard_map/all_to_all | solution.py:14
  125.2 0.3 reduce_sum.42
  125.6 0.0 slice-start
  125.6 0.8 pad_maximum_fusion.4
  126.5 12.8 %all-to-all-start.5 = ((bf16[64,8,256]{2,1,0:T(8,128)(2,1)}), bf16[64,8,256]{2,1,0:T(8,128)(2,1)S(1)}, u32[]{:S(2)}, u32[]{:S(2)}) async-start(bf16[64,8,256]{2,1,0:T(8,128)(2,1)} %pad_maximum_fusion.4), calls=%async_computation.5 | async-start | bytes 524288 | tf_op jit(solution)/shard_map/all_to_all | solution.py:14
  139.2 0.3 convolution_convert_fusion.1
  139.5 0.4 convolution_convert_fusion
  139.9 0.1 fusion.21
  140.0 2.2 %collective-permute-start.5 = (bf16[144,4,256]{2,0,1:T(8,128)(2,1)S(1)}, bf16[144,4,256]{2,0,1:T(8,128)(2,1)S(1)}, u32[]{:S(2)}, u32[]{:S(2)}) collective-permute-start(bf16[144,4,256]{2,0,1:T(8,128)(2,1)S(1)} %get-tuple-element.51), channel_id=1, source_target_pairs={{0,1},{1,2},{2,3},{3,0},{4,5},{5,6},{6,7},{7,4},{8,9},{9,10},{10,1... | collective-permute-start | bytes 884744 | tf_op jit(solution)/shard_map/ppermute | solution.py:31
  142.2 4.3 %collective-permute-start.3 = (bf16[144,4,256]{2,0,1:T(8,128)(2,1)S(1)}, bf16[144,4,256]{2,0,1:T(8,128)(2,1)S(1)}, u32[]{:S(2)}, u32[]{:S(2)}) collective-permute-start(bf16[144,4,256]{2,0,1:T(8,128)(2,1)S(1)} %get-tuple-element.52), channel_id=1, source_target_pairs={{0,3},{1,0},{2,1},{3,2},{4,7},{5,4},{6,5},{7,6},{8,11},{9,8},{10,9... | collective-permute-start | bytes 884744 | tf_op jit(solution)/shard_map/ppermute | solution.py:31
  146.5 1.9 %collective-permute-start.4 = (bf16[144,4,256]{2,0,1:T(8,128)(2,1)S(1)}, bf16[144,4,256]{2,0,1:T(8,128)(2,1)S(1)}, u32[]{:S(2)}, u32[]{:S(2)}) collective-permute-start(bf16[144,4,256]{2,0,1:T(8,128)(2,1)S(1)} %get-tuple-element.53), channel_id=1, source_target_pairs={{0,2},{1,3},{2,0},{3,1},{4,6},{5,7},{6,4},{7,5},{8,10},{9,11},{10,... | collective-permute-start | bytes 884744 | tf_op jit(solution)/shard_map/ppermute | solution.py:31
  148.4 2.8 %collective-permute-done.5 = bf16[144,4,256]{2,0,1:T(8,128)(2,1)S(1)} collective-permute-done((bf16[144,4,256]{2,0,1:T(8,128)(2,1)S(1)}, bf16[144,4,256]{2,0,1:T(8,128)(2,1)S(1)}, u32[]{:S(2)}, u32[]{:S(2)}) %collective-permute-start.5) | collective-permute-done | bytes 294944 | tf_op jit(solution)/shard_map/ppermute | solution.py:31
  151.2 1.6 collective-permute-done.3
  152.8 4.6 %collective-permute-done.4 = bf16[144,4,256]{2,0,1:T(8,128)(2,1)S(1)} collective-permute-done((bf16[144,4,256]{2,0,1:T(8,128)(2,1)S(1)}, bf16[144,4,256]{2,0,1:T(8,128)(2,1)S(1)}, u32[]{:S(2)}, u32[]{:S(2)}) %collective-permute-start.4) | collective-permute-done | bytes 294944 | tf_op jit(solution)/shard_map/ppermute | solution.py:31
  157.4 0.2 select_bitcast_fusion.3
  157.5 0.1 select_bitcast_fusion.2
  157.6 0.2 pad_maximum_fusion.1
  157.8 0.1 fusion.51
  157.9 0.3 copy.48
  158.2 1.0 squeeze.56
  159.2 0.3 copy.47
  159.6 1.0 squeeze.55
  160.6 0.3 copy.46
  160.9 1.0 squeeze.54
  161.9 18.6 %all-to-all-done.5 = bf16[64,8,256]{2,1,0:T(8,128)(2,1)S(1)} async-done(((bf16[64,8,256]{2,1,0:T(8,128)(2,1)}), bf16[64,8,256]{2,1,0:T(8,128)(2,1)S(1)}, u32[]{:S(2)}, u32[]{:S(2)}) %all-to-all-start.5) | async-done | bytes 262176 | tf_op jit(solution)/shard_map/all_to_all | solution.py:14
  180.5 0.3 convolution_convert_fusion.3
  180.8 0.6 fusion.54
  (28 shorter events, 0.4 us)
Async XLA Ops:
  0.6 32.8 %copy-start.4 = (bf16[1,48,4096]{2,1,0:T(8,128)(2,1)S(1)}, bf16[1,48,4096]{2,1,0:T(8,128)(2,1)}, u32[]{:S(2)}) copy-start(bf16[1,48,4096]{2,1,0:T(8,128)(2,1)} %param.12) | copy-start | bytes 1179652
  0.6 32.5 %copy-start.3 = (bf16[1,48,4096]{2,1,0:T(8,128)(2,1)S(1)}, bf16[1,48,4096]{2,1,0:T(8,128)(2,1)}, u32[]{:S(2)}) copy-start(bf16[1,48,4096]{2,1,0:T(8,128)(2,1)} %param.11) | copy-start | bytes 1179652
  0.7 33.0 %copy-start.5 = (bf16[1,48,4096]{2,1,0:T(8,128)(2,1)S(1)}, bf16[1,48,4096]{2,1,0:T(8,128)(2,1)}, u32[]{:S(2)}) copy-start(bf16[1,48,4096]{2,1,0:T(8,128)(2,1)} %param.13) | copy-start | bytes 1179652
  2.7 71.7 %all-to-all-start = ((bf16[64,8,256]{2,1,0:T(8,128)(2,1)}), bf16[64,8,256]{2,1,0:T(8,128)(2,1)S(1)}, u32[]{:S(2)}, u32[]{:S(2)}) async-start(bf16[64,8,256]{2,1,0:T(8,128)(2,1)} %bitcast.116), calls=%async_computation | async-start | bytes 524288 | tf_op jit(solution)/shard_map/all_to_all | solution.py:14
  34.3 10.9 %copy-start.6 = (s32[24,8]{0,1:T(8,128)S(1)}, s32[24,8]{0,1:T(8,128)}, u32[]{:S(2)}) copy-start(s32[24,8]{0,1:T(8,128)} %param.8) | copy-start | bytes 2308
  34.3 10.9 %copy-start.7 = (f32[24,8]{0,1:T(8,128)S(1)}, f32[24,8]{0,1:T(8,128)}, u32[]{:S(2)}) copy-start(f32[24,8]{0,1:T(8,128)} %param.9) | copy-start | bytes 2308
  34.5 11.3 %collective-permute-start.2 = (bf16[144,4,256]{2,0,1:T(8,128)(2,1)S(1)}, bf16[144,4,256]{2,0,1:T(8,128)(2,1)S(1)}, u32[]{:S(2)}, u32[]{:S(2)}) collective-permute-start(bf16[144,4,256]{2,0,1:T(8,128)(2,1)S(1)} %get-tuple-element.54), channel_id=1, source_target_pairs={{0,1},{1,2},{2,3},{3,0},{4,5},{5,6},{6,7},{7,4},{8,9},{9,10},{10,1... | collective-permute-start | bytes 884744 | tf_op jit(solution)/shard_map/ppermute | solution.py:31
  37.6 15.4 %collective-permute-start.1 = (bf16[144,4,256]{2,0,1:T(8,128)(2,1)S(1)}, bf16[144,4,256]{2,0,1:T(8,128)(2,1)S(1)}, u32[]{:S(2)}, u32[]{:S(2)}) collective-permute-start(bf16[144,4,256]{2,0,1:T(8,128)(2,1)S(1)} %get-tuple-element.55), channel_id=1, source_target_pairs={{0,2},{1,3},{2,0},{3,1},{4,6},{5,7},{6,4},{7,5},{8,10},{9,11},{10,... | collective-permute-start | bytes 884744 | tf_op jit(solution)/shard_map/ppermute | solution.py:31
  42.0 12.3 %collective-permute-start = (bf16[144,4,256]{2,0,1:T(8,128)(2,1)S(1)}, bf16[144,4,256]{2,0,1:T(8,128)(2,1)S(1)}, u32[]{:S(2)}, u32[]{:S(2)}) collective-permute-start(bf16[144,4,256]{2,0,1:T(8,128)(2,1)S(1)} %get-tuple-element.56), channel_id=1, source_target_pairs={{0,3},{1,0},{2,1},{3,2},{4,7},{5,4},{6,5},{7,6},{8,11},{9,8},{10,9... | collective-permute-start | bytes 884744 | tf_op jit(solution)/shard_map/ppermute | solution.py:31
  54.6 37.0 %copy-start.1 = (bf16[4,144,4,256]{3,1,2,0:T(8,128)(2,1)}, bf16[4,144,4,256]{3,1,2,0:T(8,128)(2,1)S(1)}, u32[]{:S(2)}) copy-start(bf16[4,144,4,256]{3,1,2,0:T(8,128)(2,1)S(1)} %pad_maximum_fusion) | copy-start | bytes 3538948
  92.0 17.9 %copy-start.8 = (pred[144]{0:T(512)(128)(4,1)S(1)}, pred[144]{0:T(512)(128)(4,1)}, u32[]{:S(2)}) copy-start(pred[144]{0:T(512)(128)(4,1)} %constant.125.clone.1) | copy-start | bytes 436
  101.6 8.4 %copy-start.2 = (bf16[4,144,4,256]{3,1,2,0:T(8,128)(2,1)S(1)}, bf16[4,144,4,256]{3,1,2,0:T(8,128)(2,1)}, u32[]{:S(2)}) copy-start(bf16[4,144,4,256]{3,1,2,0:T(8,128)(2,1)} %copy-done.1) | copy-start | bytes 3538948
  109.9 5.6 %copy-start = (bf16[4,144,256]{2,1,0:T(8,128)(2,1)}, bf16[4,144,256]{2,1,0:T(8,128)(2,1)S(1)}, u32[]{:S(2)}) copy-start(bf16[4,144,256]{2,1,0:T(8,128)(2,1)S(1)} %all_to_all.32) | copy-start | bytes 884740
  112.0 13.2 %all-to-all-start.4 = ((bf16[4,512,256]{2,1,0:T(8,128)(2,1)}), bf16[4,512,256]{2,1,0:T(8,128)(2,1)S(1)}, u32[]{:S(2)}, u32[]{:S(2)}) async-start(bf16[4,512,256]{2,1,0:T(8,128)(2,1)} %fusion), calls=%async_computation.4 | async-start | bytes 2097152 | tf_op jit(solution)/shard_map/all_to_all | solution.py:14
  125.6 13.9 %slice-start = ((bf16[4,144,256]{2,1,0:T(8,128)(2,1)}), bf16[4,96,256]{2,1,0:T(8,128)(2,1)S(1)}, s32[]{:S(2)}) async-start(bf16[4,144,256]{2,1,0:T(8,128)(2,1)} %copy-done), calls=%async_computation.6 | async-start | bytes 393216 | tf_op jit(solution)/shard_map/slice | solution.py:139
  126.5 54.1 %all-to-all-start.5 = ((bf16[64,8,256]{2,1,0:T(8,128)(2,1)}), bf16[64,8,256]{2,1,0:T(8,128)(2,1)S(1)}, u32[]{:S(2)}, u32[]{:S(2)}) async-start(bf16[64,8,256]{2,1,0:T(8,128)(2,1)} %pad_maximum_fusion.4), calls=%async_computation.5 | async-start | bytes 524288 | tf_op jit(solution)/shard_map/all_to_all | solution.py:14
  140.0 11.2 %collective-permute-start.5 = (bf16[144,4,256]{2,0,1:T(8,128)(2,1)S(1)}, bf16[144,4,256]{2,0,1:T(8,128)(2,1)S(1)}, u32[]{:S(2)}, u32[]{:S(2)}) collective-permute-start(bf16[144,4,256]{2,0,1:T(8,128)(2,1)S(1)} %get-tuple-element.51), channel_id=1, source_target_pairs={{0,1},{1,2},{2,3},{3,0},{4,5},{5,6},{6,7},{7,4},{8,9},{9,10},{10,1... | collective-permute-start | bytes 884744 | tf_op jit(solution)/shard_map/ppermute | solution.py:31
  142.2 10.6 %collective-permute-start.3 = (bf16[144,4,256]{2,0,1:T(8,128)(2,1)S(1)}, bf16[144,4,256]{2,0,1:T(8,128)(2,1)S(1)}, u32[]{:S(2)}, u32[]{:S(2)}) collective-permute-start(bf16[144,4,256]{2,0,1:T(8,128)(2,1)S(1)} %get-tuple-element.52), channel_id=1, source_target_pairs={{0,3},{1,0},{2,1},{3,2},{4,7},{5,4},{6,5},{7,6},{8,11},{9,8},{10,9... | collective-permute-start | bytes 884744 | tf_op jit(solution)/shard_map/ppermute | solution.py:31
  146.5 10.9 %collective-permute-start.4 = (bf16[144,4,256]{2,0,1:T(8,128)(2,1)S(1)}, bf16[144,4,256]{2,0,1:T(8,128)(2,1)S(1)}, u32[]{:S(2)}, u32[]{:S(2)}) collective-permute-start(bf16[144,4,256]{2,0,1:T(8,128)(2,1)S(1)} %get-tuple-element.53), channel_id=1, source_target_pairs={{0,2},{1,3},{2,0},{3,1},{4,6},{5,7},{6,4},{7,5},{8,10},{9,11},{10,... | collective-permute-start | bytes 884744 | tf_op jit(solution)/shard_map/ppermute | solution.py:31
